TPU v7x, 32 devices: a whole 2x2x4 slice. The times are simulated.
32 devices in a mesh: parts: 2 (over y), graph: 4 (over z), dp: 2 (over x), tensor: 2 (over core).
Axes of the slice: x: 2, y: 2, z: 4, core: 2. Of those that a mesh axis runs over, the one named last changes fastest.
Arguments:
- edges_in: bfloat16 [4, 4096, 512], P(('parts', 'dp'), 'graph', 'tensor'), parts along dimension 0, may hold values from -6 to 6
- weight: bfloat16 [512, 512], P(None, 'tensor'), may hold values from -0.25 to 0.25
- basis_tiles: bfloat16 [4, 144, 128, 128], P(('parts', 'dp'), 'graph'), parts along dimension 0, may hold values from -0.59765625 to 0.59765625
- target_blocks: int32 [4, 144], P(('parts', 'dp'), 'graph'), parts along dimension 0, may hold values from 0 to 7
- source_blocks: int32 [4, 144], P(('parts', 'dp'), 'graph'), parts along dimension 0, may hold values from 0 to 23
- counts: int32 [4, 4], P(('parts', 'dp'), 'graph'), parts along dimension 0, may hold values from 1 to 36, as said below
- grad_out: bfloat16 [4, 4096, 512], P(('parts', 'dp'), 'graph', 'tensor'), parts along dimension 0, may hold values from -6 to 6
Outputs:
- edges_out: bfloat16 [4, 4096, 512], P(('parts', 'dp'), 'graph', 'tensor'), parts along dimension 0
- grad_edges: bfloat16 [4, 4096, 512], P(('parts', 'dp'), 'graph', 'tensor'), parts along dimension 0
- grad_weight: float32 [1024, 512], P('parts', 'tensor'), parts along dimension 0
There are 2 independent parts, one for each index of `parts`. A program takes and returns all parts, laid end to end along the dimension named above; an argument that names none is the same for every part. Nothing has to cross between parts.
Inputs may be any that keep to these rules, and one draw needn't show every extreme that they name: `counts`: each shard has at least one live slot and some shard of every supercell has all 36 slots live; slots that are not live carry basis values that do not count.
All inputs are finite; a program needn't handle non-finite values.
Results may differ from a plain program's by a relative error of at most 0.0095.
Values may be sent and summed in bfloat16 or wider, within the bound.
No kernel may reach another device: no remote copies, remote signals or barrier semaphores. Data moves between devices by JAX's collectives and lax.ppermute only.
A program may use at most 64 MiB of HBM per device.

v0:
```python
import jax
import jax.numpy as jnp
from jax import lax
from jax.sharding import PartitionSpec as P


def padded(cells, sides, width):
    for axis, dim in sides:
        count = lax.axis_size(axis)
        head = lax.slice_in_dim(cells, 0, width, axis=dim)
        tail = lax.slice_in_dim(cells, cells.shape[dim] - width, cells.shape[dim], axis=dim)
        cells = jnp.concatenate(
            [
                lax.ppermute(tail, axis, [(i, (i + 1) % count) for i in range(count)]),
                cells,
                lax.ppermute(head, axis, [((i + 1) % count, i) for i in range(count)]),
            ],
            axis=dim,
        )
    return cells


def from_behind(value, axis, steps):
    count = lax.axis_size(axis)
    pairs = [(source, (source + steps) % count) for source in range(count)]
    return lax.ppermute(value, axis, pairs)


def slope_factor(preact):
    sig = jax.nn.sigmoid(preact)
    return sig * (1.0 + preact * (1.0 - sig))


def shards(edges_in, weight, basis_tiles, target_blocks, source_blocks, counts, grad_out):
    edge_rows = edges_in.shape[1]
    chans = edges_in.shape[2]
    tile_rows = basis_tiles.shape[2]
    nblocks = edge_rows // tile_rows
    slots = basis_tiles.shape[1]
    full_rows = lax.all_gather(edges_in, "tensor", axis=2, tiled=True)[0]
    preact = jnp.dot(full_rows, weight, preferred_element_type=jnp.float32)
    activated = jax.nn.silu(preact).astype(jnp.bfloat16)
    widened = padded(activated, (("graph", 0),), edge_rows)
    wide_blocks = widened.reshape(3 * nblocks, tile_rows, chans)
    tiles = basis_tiles[0]
    target = target_blocks[0]
    source = source_blocks[0]
    live = (jnp.arange(slots, dtype=jnp.int32) < counts[0, 0]).astype(jnp.float32)
    to_target = (target[:, None] == jnp.arange(nblocks, dtype=jnp.int32)[None, :]).astype(
        jnp.float32
    ) * live[:, None]
    to_source = (source[:, None] == jnp.arange(3 * nblocks, dtype=jnp.int32)[None, :]).astype(
        jnp.float32
    ) * live[:, None]
    picked = wide_blocks[source]
    contrib = jnp.einsum("kij,kjc->kic", tiles, picked, preferred_element_type=jnp.float32)
    triplet = jnp.einsum(
        "kt,kic->tic", to_target, contrib, precision=lax.Precision.HIGHEST
    ).reshape(edge_rows, chans)
    edges_out = (edges_in[0].astype(jnp.float32) + triplet).astype(jnp.bfloat16)
    g_rows = grad_out[0]
    g_picked = g_rows.reshape(nblocks, tile_rows, chans)[target]
    back_terms = jnp.einsum("kji,kjc->kic", tiles, g_picked, preferred_element_type=jnp.float32)
    back_wide = jnp.einsum("ks,kic->sic", to_source, back_terms, precision=lax.Precision.HIGHEST)
    from_next = from_behind(back_wide[:nblocks], "graph", -1)
    from_prev = from_behind(back_wide[2 * nblocks :], "graph", 1)
    back = (back_wide[nblocks : 2 * nblocks] + from_next + from_prev).reshape(edge_rows, chans)
    slope = (back * slope_factor(preact)).astype(jnp.bfloat16)
    partial_terms = jnp.dot(slope, weight.T, preferred_element_type=jnp.float32)
    input_terms = lax.psum_scatter(
        partial_terms.astype(jnp.bfloat16), "tensor", scatter_dimension=1, tiled=True
    ).astype(jnp.float32)
    grad_edges = (g_rows.astype(jnp.float32) + input_terms).astype(jnp.bfloat16)
    weight_part = jnp.dot(full_rows.T, slope, preferred_element_type=jnp.float32)
    total = lax.psum(weight_part, ("graph", "dp"))
    scale = jnp.sqrt(
        jnp.float32(lax.axis_size("dp") * edges_in.shape[0] * lax.axis_size("graph") * edge_rows)
    )
    return (edges_out[None], grad_edges[None], total / scale)


def solution(mesh):
    placed = (
        P(("parts", "dp"), "graph", "tensor"),
        P(None, "tensor"),
        P(("parts", "dp"), "graph", None, None),
        P(("parts", "dp"), "graph"),
        P(("parts", "dp"), "graph"),
        P(("parts", "dp"), "graph"),
        P(("parts", "dp"), "graph", "tensor"),
    )
    return jax.shard_map(
        shards,
        mesh=mesh,
        in_specs=placed,
        out_specs=(
            P(("parts", "dp"), "graph", "tensor"),
            P(("parts", "dp"), "graph", "tensor"),
            P("parts", "tensor"),
        ),
        check_vma=False,
    )
```

profile of v0, /device:TPU:0, one launch (start us, length us, event | category | flops | bytes accessed | tf_op | source)
XLA Modules:
  0.0 195.6 jit_solution(436048163772336791)
XLA Ops:
  8.6 1.7 gather_fusion.1
  10.4 3.0 %fusion.4 = f32[36,256,128]{2,1,0:T(8,128)} fusion(bf16[36,128,256]{2,1,0:T(8,128)(2,1)S(1)} %gather_fusion.1, bf16[1,36,128,128]{3,2,1,0:T(8,128)(2,1)S(1)} %copy-done), kind=kOutput, calls=%fused_computation.9 | convolution fusion | flops 301989888 | bytes 8257536 | tf_op jit(solution)/shard_map/kji,kjc->kic/dot_general | solution.py:63
  13.4 6.0 %copy.16 = f32[36,256,128]{1,0,2:T(8,128)} copy(f32[36,256,128]{2,1,0:T(8,128)} %fusion.4) | data formatting | bytes 9437184 | tf_op jit(solution)/shard_map/kji,kjc->kic/dot_general | solution.py:63
  19.4 4.8 %fusion = f32[24,128,256]{2,0,1:T(8,128)S(1)} fusion(f32[36,256,128]{1,0,2:T(8,128)} %copy.16, f32[36]{0:T(128)S(1)} %compare_convert_fusion, s32[36]{0:T(128)S(1)} %bitcast.63), kind=kOutput, calls=%fused_computation.2 | convolution fusion | flops 339740352 | bytes 7864608 | tf_op jit(solution)/shard_map/ks,kic->sic/dot_general | solution.py:64
  24.2 1.6 copy-done.2
  25.8 1.2 fusion.30
  27.0 5.1 %collective-permute-start.2 = (f32[8,128,256]{2,0,1:T(8,128)}, f32[8,128,256]{2,0,1:T(8,128)S(1)}, u32[]{:S(2)}, u32[]{:S(2)}) collective-permute-start(f32[8,128,256]{2,0,1:T(8,128)} %get-tuple-element.9), channel_id=1, source_target_pairs={{0,12},{4,0},{8,4},{12,8},{1,13},{5,1},{9,5},{13,9},{2,14},{6,2},{... | collective-permute-start | bytes 3145736 | tf_op jit(solution)/shard_map/ppermute | solution.py:26
  32.1 23.8 %collective-permute-done.2 = f32[8,128,256]{2,0,1:T(8,128)S(1)} collective-permute-done((f32[8,128,256]{2,0,1:T(8,128)}, f32[8,128,256]{2,0,1:T(8,128)S(1)}, u32[]{:S(2)}, u32[]{:S(2)}) %collective-permute-start.2) | collective-permute-done | bytes 1048608 | tf_op jit(solution)/shard_map/ppermute | solution.py:26
  55.9 22.2 %collective-permute-done.3 = f32[8,128,256]{2,0,1:T(8,128)} collective-permute-done((f32[8,128,256]{2,0,1:T(8,128)S(1)}, f32[8,128,256]{2,0,1:T(8,128)}, u32[]{:S(2)}, u32[]{:S(2)}) %collective-permute-start.3) | collective-permute-done | bytes 1048608 | tf_op jit(solution)/shard_map/ppermute | solution.py:26
  78.1 1.7 fusion.8
  80.3 1.9 fusion.10
  82.2 1.3 convolution_bitcast_fusion
  83.6 1.4 convolution_convert_fusion
  85.0 1.6 collective-permute-start.1
  87.1 76.1 %all-reduce.2.cloned.1.call-done = f32[512,256]{0,1:T(8,128)} async-done(((f32[512,256]{0,1:T(8,128)}), f32[512,256]{0,1:T(8,128)}) %all-reduce.2.cloned.1.call-update) | async-done | bytes 524304 | tf_op jit(solution)/shard_map/psum | solution.py:75
  163.2 1.1 broadcast_multiply_fusion
  164.3 1.0 copy.14
  166.1 1.3 pad_maximum_fusion
  167.4 2.3 %gather_fusion = bf16[36,128,256]{2,1,0:T(8,128)(2,1)} fusion(bf16[24,128,256]{2,1,0:T(8,128)(2,1)S(1)} %bitcast.61, s32[1024]{0:T(1024)S(1)} %pad_clamp_fusion.1), kind=kCustom, calls=%fused_computation | custom fusion | bytes 4718736 | tf_op jit(solution)/shard_map/gather | solution.py:55
  169.7 5.0 %fusion.6 = f32[36,256,128]{2,1,0:T(8,128)} fusion(bf16[36,128,256]{2,1,0:T(8,128)(2,1)} %gather_fusion, bf16[1,36,128,128]{3,2,1,0:T(8,128)(2,1)S(1)} %copy-done), kind=kOutput, calls=%fused_computation.11 | convolution fusion | flops 301989888 | bytes 8257536 | tf_op jit(solution)/shard_map/kij,kjc->kic/dot_general | solution.py:56
  174.7 6.0 %copy.15 = f32[36,256,128]{1,0,2:T(8,128)} copy(f32[36,256,128]{2,1,0:T(8,128)} %fusion.6) | data formatting | bytes 9437184 | tf_op jit(solution)/shard_map/kij,kjc->kic/dot_general | solution.py:56
  180.7 4.5 %fusion.2 = f32[8,128,256]{2,0,1:T(8,128)S(1)} fusion(f32[36,256,128]{1,0,2:T(8,128)} %copy.15, f32[36]{0:T(128)S(1)} %compare_convert_fusion, s32[36]{0:T(128)S(1)} %bitcast.64), kind=kOutput, calls=%fused_computation.4 | convolution fusion | flops 113246784 | bytes 5767456 | tf_op jit(solution)/shard_map/kt,kic->tic/dot_general | solution.py:57
  186.2 0.9 fusion.11
  187.1 2.0 %fusion.15 = bf16[1,1024,256]{2,1,0:T(8,128)(2,1)} fusion(bf16[1024,256]{1,0:T(8,128)(2,1)} %reduce-scatter.2.cloned.1.call-done, bf16[1,1024,256]{2,1,0:T(8,128)(2,1)S(1)} %copy-done.1), kind=kLoop, calls=%fused_computation.26 | loop fusion | flops 1048576 | bytes 1572864 | tf_op jit(solution)/shard_map/broadcast_in_dim | solution.py:79
  (36 shorter events, 3.6 us)
Async XLA Ops:
  7.2 3.2 %copy-start = (bf16[1,36,128,128]{3,2,1,0:T(8,128)(2,1)S(1)}, bf16[1,36,128,128]{3,2,1,0:T(8,128)(2,1)}, u32[]{:S(2)}) copy-start(bf16[1,36,128,128]{3,2,1,0:T(8,128)(2,1)} %param.9) | copy-start | bytes 3538948
  7.2 73.1 %all-gather.2.cloned.1.call-start = ((), (), s32[]{:S(2)}) async-start(), calls=%async_computation.1 | async-start | bytes 1572864 | tf_op jit(solution)/shard_map/all_gather | solution.py:40
  13.4 6.0 %copy-start.7 = (s32[1,36]{1,0:T(1,128)S(1)}, s32[1,36]{1,0:T(1,128)}, u32[]{:S(2)}) copy-start(s32[1,36]{1,0:T(1,128)} %param.11) | copy-start | bytes 436
  24.2 1.6 copy-start.2
  27.0 28.9 %collective-permute-start.2 = (f32[8,128,256]{2,0,1:T(8,128)}, f32[8,128,256]{2,0,1:T(8,128)S(1)}, u32[]{:S(2)}, u32[]{:S(2)}) collective-permute-start(f32[8,128,256]{2,0,1:T(8,128)} %get-tuple-element.9), channel_id=1, source_target_pairs={{0,12},{4,0},{8,4},{12,8},{1,13},{5,1},{9,5},{13,9},{2,14},{6,2},{... | collective-permute-start | bytes 3145736 | tf_op jit(solution)/shard_map/ppermute | solution.py:26
  32.0 46.1 %collective-permute-start.3 = (f32[8,128,256]{2,0,1:T(8,128)S(1)}, f32[8,128,256]{2,0,1:T(8,128)}, u32[]{:S(2)}, u32[]{:S(2)}) collective-permute-start(f32[8,128,256]{2,0,1:T(8,128)S(1)} %get-tuple-element.10), channel_id=1, source_target_pairs={{0,4},{4,8},{8,12},{12,0},{1,5},{5,9},{9,13},{13,1},{2,6},{6,10},{... | collective-permute-start | bytes 3145736 | tf_op jit(solution)/shard_map/ppermute | solution.py:26
  32.1 48.2 %copy-start.6 = (bf16[512,256]{1,0:T(8,128)(2,1)S(1)}, bf16[512,256]{1,0:T(8,128)(2,1)}, u32[]{:S(2)}) copy-start(bf16[512,256]{1,0:T(8,128)(2,1)} %param.8) | copy-start | bytes 786436
  32.1 131.1 %all-reduce.2.cloned.1.call-start = ((), (), s32[]{:S(2)}) async-start(), calls=%async_computation.3 | async-start | bytes 1048576 | tf_op jit(solution)/shard_map/psum | solution.py:75
  80.3 1.9 copy-start.4
  83.5 103.6 %reduce-scatter.2.cloned.1.call-start = ((), (), s32[]{:S(2)}) async-start(), calls=%async_computation.2 | async-start | bytes 1572864 | tf_op jit(solution)/shard_map/reduce_scatter | solution.py:70
  85.0 80.3 %collective-permute-start.1 = (bf16[1024,256]{1,0:T(8,128)(2,1)S(1)}, bf16[1024,256]{1,0:T(8,128)(2,1)S(1)}, u32[]{:S(2)}, u32[]{:S(2)}) collective-permute-start(bf16[1024,256]{1,0:T(8,128)(2,1)S(1)} %get-tuple-element.12), channel_id=1, source_target_pairs={{4,0},{8,4},{12,8},{0,12},{5,1},{9,5},{13,9},{1,13},{6,2},{10,6},{... | collective-permute-start | bytes 1572872 | tf_op jit(solution)/shard_map/ppermute | solution.py:16
  86.6 79.5 %collective-permute-start = (bf16[1024,256]{1,0:T(8,128)(2,1)S(1)}, bf16[1024,256]{1,0:T(8,128)(2,1)}, u32[]{:S(2)}, u32[]{:S(2)}) collective-permute-start(bf16[1024,256]{1,0:T(8,128)(2,1)S(1)} %get-tuple-element.12), channel_id=1, source_target_pairs={{0,4},{4,8},{8,12},{12,0},{1,5},{5,9},{9,13},{13,1},{2,6},{6,10},{... | collective-permute-start | bytes 1572872 | tf_op jit(solution)/shard_map/ppermute | solution.py:14
  165.3 0.8 copy-start.5
  174.7 6.0 %copy-start.8 = (s32[1,36]{1,0:T(1,128)S(1)}, s32[1,36]{1,0:T(1,128)}, u32[]{:S(2)}) copy-start(s32[1,36]{1,0:T(1,128)} %param.10) | copy-start | bytes 436
  185.2 1.0 copy-start.3
  185.2 1.9 copy-start.1
Sparse Core Ops, SparseCore 0:
  32.2 10.4 all-gather.1
  83.6 79.5 all-reduce.1
  165.5 7.8 reduce-scatter.1
where the time goes:
time: 196 us
  waiting for transfers between devices  122 us (62%)
  local copies, waits for them, and re-layouts  21.9 us (11%)
  matrix products  21.9 us (11%)
  between operations  14.6 us (7%)
  other arithmetic  7.69 us (4%)
  starting transfers between devices  7.25 us (4%)
    psum x1, waiting for transfers between devices, shards(): total = lax.psum(weight_part, ('graph', 'dp'))  76.1 us
    ppermute x2, waiting for transfers between devices, from_behind(): return lax.ppermute(value, axis, pairs)  46 us
    dot_general x1, local copies, waits for them, and re-layouts, shards(): jnp.einsum('kij,kjc->kic', tiles, picked, preferred_element_type=jnp.floa...  5.96 us
    dot_general x1, local copies, waits for them, and re-layouts, shards(): jnp.einsum('kji,kjc->kic', tiles, g_picked, preferred_element_type=jnp.fl...  5.96 us
    ppermute x2, starting transfers between devices, from_behind(): return lax.ppermute(value, axis, pairs)  5.05 us
    dot_general x1, matrix products, shards(): jnp.einsum('kij,kjc->kic', tiles, picked, preferred_element_type=jnp.floa...  5.01 us
    dot_general x1, matrix products, shards(): jnp.einsum('ks,kic->sic', to_source, back_terms, precision=lax.Precision....  4.81 us
    dot_general x1, matrix products, shards(): jnp.einsum('kt,kic->tic', to_target, contrib, precision=lax.Precision.HIG...  4.47 us
  transfers between devices with their start and end apart: 7, of which 3 were waited for; matrix products, arithmetic and copies ran while one was open for 13% of the time, Pallas kernels for 0%

commit v1 on v0

v1 whole, which is shorter than its diff:
```python
import functools

import jax
import jax.numpy as jnp
from jax import lax
from jax.experimental import pallas as pl
from jax.experimental.pallas import tpu as pltpu
from jax.sharding import PartitionSpec as P

F32 = jnp.float32
BF16 = jnp.bfloat16
UNROLL = 4
VMEM = pl.BlockSpec(memory_space=pltpu.VMEM)
SMEM = pl.BlockSpec(memory_space=pltpu.SMEM)


def call(body, ins, outs, scratch=(), flops=0, nbytes=0):
    return pl.pallas_call(
        body,
        in_specs=[SMEM if x.dtype == jnp.int32 else VMEM for x in ins],
        out_shape=[jax.ShapeDtypeStruct(s, d) for s, d in outs],
        out_specs=[VMEM for _ in outs],
        scratch_shapes=list(scratch),
        cost_estimate=pl.CostEstimate(flops=flops, bytes_accessed=nbytes, transcendentals=0),
        compiler_params=pltpu.CompilerParams(vmem_limit_bytes=32 * 1024 * 1024),
    )(*ins)


def shift(value, axis, steps):
    count = lax.axis_size(axis)
    return lax.ppermute(value, axis, [(i, (i + steps) % count) for i in range(count)])


def pick(listed, count, source, low, high):
    slots = source.shape[1]

    def step(k, found):
        listed[found] = k
        s = source[0, k]
        inside = (k < count) & (s >= low) & (s < high)
        return found + inside.astype(jnp.int32)

    found = lax.fori_loop(0, slots, step, jnp.int32(0))
    for j in range(UNROLL):
        listed[found + j] = 0
    return found


def over_tiles(listed, found, step):
    def some(i, carry):
        for j in range(UNROLL):
            at = i * UNROLL + j
            step(listed[at], at < found)
        return carry

    lax.fori_loop(0, (found + UNROLL - 1) // UNROLL, some, 0)


def back_body(ranges, nblocks, counts, target, source, tiles, grads, *rest):
    n = len(ranges)
    outs, acc, listed = rest[:n], rest[n], rest[n + 1]
    for (low, base), out in zip(ranges, outs):
        acc[...] = jnp.zeros_like(acc)
        found = pick(listed, counts[0, 0], source, low, low + nblocks)

        def step(k, valid):
            at = jnp.where(valid, source[0, k] - low, nblocks)
            acc[at] += lax.dot_general(
                tiles[k], grads[target[0, k]], (((0,), (0,)), ((), ())), preferred_element_type=F32
            )

        over_tiles(listed, found, step)
        for b in range(nblocks):
            out[b] = acc[b].astype(out.dtype)


def triplet_body(low, nblocks, counts, target, source, tiles, rows, start, out, acc, listed):
    for b in range(nblocks):
        acc[b] = start[b].astype(F32)
    found = pick(listed, counts[0, 0], source, low, low + nblocks)

    def step(k, valid):
        at = jnp.where(valid, target[0, k], nblocks)
        s = jnp.where(valid, source[0, k] - low, 0)
        acc[at] += jnp.dot(tiles[k], rows[s], preferred_element_type=F32)

    over_tiles(listed, found, step)
    for b in range(nblocks):
        out[b] = acc[b].astype(out.dtype)


def preact_body(step, mine, theirs, weight, act, factor, flipped):
    rows, chans = mine.shape
    core = lax.axis_index("tensor")
    own = pl.ds(pl.multiple_of(core * chans, chans), chans)
    other = pl.ds(pl.multiple_of((1 - core) * chans, chans), chans)
    for r in range(0, rows, step):
        at = pl.ds(r, step)
        pre = jnp.dot(mine[at], weight[own], preferred_element_type=F32) + jnp.dot(
            theirs[at], weight[other], preferred_element_type=F32
        )
        sig = 1.0 / (1.0 + jnp.exp(-pre))
        act[at] = (pre * sig).astype(BF16)
        factor[at] = sig * (1.0 + pre * (1.0 - sig))
        flipped[own, at] = mine[at].T
        flipped[other, at] = theirs[at].T


def slope_body(step, ndp, back, from_next, from_prev, factor, grads, weight, flipped, *rest):
    to_core, gsum, keep = rest[:3]
    sends = rest[3 : 2 + ndp]
    slope, part = rest[2 + ndp :]
    rows, chans = grads.shape
    core = lax.axis_index("tensor")
    own = pl.ds(pl.multiple_of(core * chans, chans), chans)
    other = pl.ds(pl.multiple_of((1 - core) * chans, chans), chans)
    last = (((1,), (1,)), ((), ()))
    for r in range(0, rows, step):
        at = pl.ds(r, step)
        total = back[at] + from_next[at].astype(F32) + from_prev[at].astype(F32)
        piece = (total * factor[at]).astype(BF16)
        slope[at] = piece
        to_core[at] = lax.dot_general(piece, weight[other], last, preferred_element_type=F32).astype(BF16)
        gsum[at] = grads[at].astype(F32) + lax.dot_general(
            piece, weight[own], last, preferred_element_type=F32
        )
    part[...] = jnp.dot(flipped[...], slope[...], preferred_element_type=F32)
    dp = lax.axis_index("dp")
    size = keep.shape[0]
    keep[...] = part[pl.ds(pl.multiple_of(dp * size, size), size)]
    for j, send in enumerate(sends):
        to = lax.rem(dp + j + 1, ndp)
        send[...] = part[pl.ds(pl.multiple_of(to * size, size), size)].astype(BF16)


def grads_body(gsum, arrived, out):
    out[...] = (gsum[...] + arrived[...].astype(F32)).astype(BF16)


def scatter_body(ndp, nz, kept, *rest):
    arrived = rest[: ndp - 1]
    keep = rest[ndp - 1]
    sends = rest[ndp : ndp + nz - 1]
    part = rest[ndp + nz - 1]
    total = kept[...]
    for ref in arrived:
        total = total + ref[...].astype(F32)
    part[...] = total
    z = lax.axis_index("graph")
    size = keep.shape[0]
    keep[...] = part[pl.ds(pl.multiple_of(z * size, size), size)]
    for j, send in enumerate(sends):
        to = lax.rem(z + j + 1, nz)
        send[...] = part[pl.ds(pl.multiple_of(to * size, size), size)].astype(BF16)


def total_body(scale, nz, kept, *rest):
    total = kept[...]
    for ref in rest[: nz - 1]:
        total = total + ref[...].astype(F32)
    rest[nz - 1][...] = (total * scale).astype(BF16)


def gather_body(axis, count, *refs):
    out = refs[count]
    me = lax.axis_index(axis)
    size = refs[0].shape[0]
    for j in range(count):
        at = lax.rem(me - j + count, count)
        out[pl.ds(pl.multiple_of(at * size, size), size)] = refs[j][...].astype(out.dtype)


def weight_total(keep, sends, scale):
    ndp, nz = lax.axis_size("dp"), lax.axis_size("graph")
    size, chans = keep.shape
    arrived = [shift(s, "dp", j + 1) for j, s in enumerate(sends)]
    part = size // nz
    parts = call(
        functools.partial(scatter_body, ndp, nz),
        [keep, *arrived],
        [((part, chans), F32)] + [((part, chans), BF16)] * (nz - 1),
        [pltpu.VMEM((size, chans), F32)],
    )
    arrived = [shift(s, "graph", j + 1) for j, s in enumerate(parts[1:])]
    (mine,) = call(
        functools.partial(total_body, scale, nz), [parts[0], *arrived], [((part, chans), BF16)]
    )
    arrived = [shift(mine, "graph", j + 1) for j in range(nz - 1)]
    (wide,) = call(
        functools.partial(gather_body, "graph", nz), [mine, *arrived], [((size, chans), BF16)]
    )
    arrived = [shift(wide, "dp", j + 1) for j in range(ndp - 1)]
    (full,) = call(
        functools.partial(gather_body, "dp", ndp), [wide, *arrived], [((size * ndp, chans), F32)]
    )
    return full


def shards(edges_in, weight, basis_tiles, target_blocks, source_blocks, counts, grad_out):
    rows, chans = edges_in.shape[1], edges_in.shape[2]
    tile = basis_tiles.shape[2]
    nblocks = rows // tile
    slots = basis_tiles.shape[1]
    depth = weight.shape[0]
    ndp, nz = lax.axis_size("dp"), lax.axis_size("graph")
    mine, grads, tiles = edges_in[0], grad_out[0], basis_tiles[0]
    blocks = (nblocks, tile, chans)
    flat = (rows, chans)
    index = [counts, target_blocks, source_blocks, tiles]
    work = [pltpu.VMEM((nblocks + 1, tile, chans), F32), pltpu.SMEM((slots + UNROLL,), jnp.int32)]
    unit = 2 * tile * tile * chans * slots // 3

    theirs = shift(mine, "tensor", 1)
    to_prev, to_next = call(
        functools.partial(back_body, ((0, 0), (2 * nblocks, 0)), nblocks),
        [*index, grads.reshape(blocks)],
        [(blocks, BF16), (blocks, BF16)],
        work,
        flops=2 * unit,
        nbytes=4 * rows * chans,
    )
    from_next = shift(to_prev, "graph", -1)
    from_prev = shift(to_next, "graph", 1)
    (back,) = call(
        functools.partial(back_body, ((nblocks, 0),), nblocks),
        [*index, grads.reshape(blocks)],
        [(blocks, F32)],
        work,
        flops=unit,
        nbytes=4 * rows * chans,
    )
    act, factor, flipped = call(
        functools.partial(preact_body, 256),
        [mine, theirs, weight],
        [(flat, BF16), (flat, F32), ((depth, rows), BF16)],
        flops=2 * rows * depth * chans,
        nbytes=8 * rows * chans,
    )
    act_prev = shift(act, "graph", 1)
    act_next = shift(act, "graph", -1)
    (acc,) = call(
        functools.partial(triplet_body, nblocks, nblocks),
        [*index, act.reshape(blocks), mine.reshape(blocks)],
        [(blocks, F32)],
        work,
        flops=unit,
        nbytes=4 * rows * chans,
    )
    size = depth // ndp
    to_core, gsum, keep, *sends = call(
        functools.partial(slope_body, 256, ndp),
        [back.reshape(flat), from_next.reshape(flat), from_prev.reshape(flat), factor, grads, weight, flipped],
        [(flat, BF16), (flat, F32), ((size, chans), F32)] + [((size, chans), BF16)] * (ndp - 1),
        [pltpu.VMEM(flat, BF16), pltpu.VMEM((depth, chans), F32)],
        flops=4 * rows * depth * chans,
        nbytes=8 * rows * chans,
    )
    arrived = shift(to_core, "tensor", 1)
    (grad_edges,) = call(grads_body, [gsum, arrived], [(flat, BF16)], nbytes=8 * rows * chans)
    scale = float(1.0 / (ndp * edges_in.shape[0] * nz * rows) ** 0.5)
    if size % (16 * nz) == 0:
        grad_weight = weight_total(keep, sends, scale)
    else:
        grad_weight = wide_total(keep, sends, scale)
    (acc,) = call(
        functools.partial(triplet_body, 0, nblocks),
        [*index, act_prev.reshape(blocks), acc],
        [(blocks, F32)],
        work,
        flops=unit,
        nbytes=4 * rows * chans,
    )
    (edges_out,) = call(
        functools.partial(triplet_body, 2 * nblocks, nblocks),
        [*index, act_next.reshape(blocks), acc],
        [(blocks, BF16)],
        work,
        flops=unit,
        nbytes=4 * rows * chans,
    )
    return edges_out.reshape(1, rows, chans), grad_edges[None], grad_weight


def wide_total(keep, sends, scale):
    ndp = lax.axis_size("dp")
    total = keep
    for j, s in enumerate(sends):
        total = total + shift(s, "dp", j + 1).astype(F32)
    total = (lax.psum(total, "graph") * scale).astype(BF16)
    return lax.all_gather(total, "dp", axis=0, tiled=True).astype(F32)


def solution(mesh):
    placed = (
        P(("parts", "dp"), "graph", "tensor"),
        P(None, "tensor"),
        P(("parts", "dp"), "graph", None, None),
        P(("parts", "dp"), "graph"),
        P(("parts", "dp"), "graph"),
        P(("parts", "dp"), "graph"),
        P(("parts", "dp"), "graph", "tensor"),
    )
    return jax.shard_map(
        shards,
        mesh=mesh,
        in_specs=placed,
        out_specs=(
            P(("parts", "dp"), "graph", "tensor"),
            P(("parts", "dp"), "graph", "tensor"),
            P("parts", "tensor"),
        ),
        check_vma=False,
    )
```

time: 196 us -> 85.6 us (0.44)
  waiting for transfers between devices: 122 us -> 45.6 us
  matrix products: 21.9 us -> 0 us
  local copies, waits for them, and re-layouts: 21.9 us -> 3.64 us
  Pallas kernels: 0 us -> 14.5 us
  starting transfers between devices: 7.25 us -> 20.8 us
  between operations: 14.6 us -> 1.41 us
  other arithmetic: 7.69 us -> 0 us
    psum x1 -> x0, waiting for transfers between devices: 76.1 us -> none  [shards(): total = lax.psum(weight_part, ('graph', 'dp'))]
    dot_general x7 -> x0, matrix products: 21.9 us -> none  [the longest x1 5.01 us: shards(): jnp.einsum('kij,kjc->kic', tiles, picked, preferred_element_type=jnp.floa...]
    pallas_call x0 -> x12, Pallas kernels: none -> 14.5 us  [call(): pl.pallas_call(body, in_specs=[SMEM if x.dtype == jnp.int32 else VMEM for...]
    ppermute x4 -> x14, starting transfers between devices: 7.13 us -> 20.8 us  [shift(): lax.ppermute(value, axis, [(i, (i + steps) % count) for i in range(count)])]
    dot_general x3 -> x0, local copies, waits for them, and re-layouts: 12.3 us -> none  [the longest x1 5.96 us: shards(): jnp.einsum('kij,kjc->kic', tiles, picked, preferred_element_type=jnp.floa...]
    gather x2 -> x0, local copies, waits for them, and re-layouts: 4.05 us -> none  [the longest x1 2.31 us: shards(): picked = wide_blocks[source]]
    broadcast_in_dim x1 -> x0, other arithmetic: 1.96 us -> none  [shards(): return (edges_out[None], grad_edges[None], total / scale)]
    unnamed x19 -> x20, local copies, waits for them, and re-layouts: 4.14 us -> 3.64 us
  transfers between devices with their start and end apart: 7 -> 14, of which waited for: 3 -> 8; matrix products, arithmetic and copies ran while one was open for 13% -> 0% of each run, Pallas kernels for 0% -> 16%
where the time goes in v1:
time: 85.6 us; the launch traced here: 86 us
  waiting for transfers between devices  45.6 us (53%)
  starting transfers between devices  20.8 us (24%)
  Pallas kernels  14.5 us (17%)
  local copies, waits for them, and re-layouts  3.64 us (4%)
  between operations  1.41 us (2%)
    ppermute x14, waiting for transfers between devices, shift(): lax.ppermute(value, axis, [(i, (i + steps) % count) for i in range(count)])  45.6 us
    ppermute x14, starting transfers between devices, shift(): lax.ppermute(value, axis, [(i, (i + steps) % count) for i in range(count)])  20.8 us
    pallas_call x12, Pallas kernels, call(): pl.pallas_call(body, in_specs=[SMEM if x.dtype == jnp.int32 else VMEM for...  14.5 us
    unnamed x20, local copies, waits for them, and re-layouts  3.64 us
  transfers between devices with their start and end apart: 14, of which 8 were waited for; matrix products, arithmetic and copies ran while one was open for 0% of the time, Pallas kernels for 16%

profile of v1, /device:TPU:0, one launch (start us, length us, event | category | flops | bytes accessed | tf_op | source)
XLA Modules:
  0.0 86.0 jit_solution(2751777866997386273)
XLA Ops:
  1.8 1.3 %copy-done = bf16[1,36,128,128]{3,2,1,0:T(8,128)(2,1)S(1)} copy-done((bf16[1,36,128,128]{3,2,1,0:T(8,128)(2,1)S(1)}, bf16[1,36,128,128]{3,2,1,0:T(8,128)(2,1)}, u32[]{:S(2)}) %copy-start) | copy-done | bytes 1179672
  3.1 1.0 %copy-done.2 = bf16[1,1024,256]{2,1,0:T(8,128)(2,1)S(1)} copy-done((bf16[1,1024,256]{2,1,0:T(8,128)(2,1)S(1)}, bf16[1,1024,256]{2,1,0:T(8,128)(2,1)}, u32[]{:S(2)}) %copy-start.2) | copy-done | bytes 524312
  5.4 3.0 %shard_map.99 = (bf16[8,128,256]{2,1,0:T(8,128)(2,1)S(1)}, bf16[8,128,256]{2,1,0:T(8,128)(2,1)S(1)}) custom-call(s32[1,1]{1,0:T(1,128)S(6)} %copy.10.counts, s32[1,36]{1,0:T(1,128)S(1)} %copy-done.6, s32[1,36]{1,0:T(1,128)S(1)} %copy-done.8, bf16[36,128,128]{2,1,0:T(8,128)(2,1)S(1)} %bitcast.13, bf16[8,128,256]{2,1,0:T(8,128)(2,1)S(1)} %bitcast.18), custom_call_target="tpu_custom_call" | custom-call | flops 201326592 | bytes 1048576 | tf_op jit(solution)/shard_map/pallas_call | solution.py:18
  8.4 4.1 %collective-permute-start.3 = (bf16[8,128,256]{2,1,0:T(8,128)(2,1)S(1)}, bf16[8,128,256]{2,1,0:T(8,128)(2,1)S(1)}, u32[]{:S(2)}, u32[]{:S(2)}) collective-permute-start(bf16[8,128,256]{2,1,0:T(8,128)(2,1)S(1)} %get-tuple-element.17), channel_id=1, source_target_pairs={{0,12},{4,0},{8,4},{12,8},{1,13},{5,1},{9,5},{13,9},{2,14},{6,2},{... | collective-permute-start | bytes 1572872 | tf_op jit(solution)/shard_map/ppermute | solution.py:31
  12.6 2.1 %shard_map.98 = f32[8,128,256]{2,1,0:T(8,128)S(1)} custom-call(s32[1,1]{1,0:T(1,128)S(6)} %copy.10.counts, s32[1,36]{1,0:T(1,128)S(1)} %copy-done.6, s32[1,36]{1,0:T(1,128)S(1)} %copy-done.8, bf16[36,128,128]{2,1,0:T(8,128)(2,1)S(1)} %bitcast.14, bf16[8,128,256]{2,1,0:T(8,128)(2,1)S(1)} %bitcast.19), custom_call_target="tpu_custom_call" | custom-call | flops 100663296 | bytes 1048576 | tf_op jit(solution)/shard_map/pallas_call | solution.py:18
  15.4 3.1 %collective-permute-start.1 = (bf16[1024,256]{1,0:T(8,128)(2,1)S(1)}, bf16[1024,256]{1,0:T(8,128)(2,1)S(1)}, u32[]{:S(2)}, u32[]{:S(2)}) collective-permute-start(bf16[1024,256]{1,0:T(8,128)(2,1)S(1)} %get-tuple-element.16), channel_id=1, source_target_pairs={{0,12},{4,0},{8,4},{12,8},{1,13},{5,1},{9,5},{13,9},{2,14},{6,2},{... | collective-permute-start | bytes 1572872 | tf_op jit(solution)/shard_map/ppermute | solution.py:31
  18.5 6.4 %collective-permute-done.3 = bf16[8,128,256]{2,1,0:T(8,128)(2,1)S(1)} collective-permute-done((bf16[8,128,256]{2,1,0:T(8,128)(2,1)S(1)}, bf16[8,128,256]{2,1,0:T(8,128)(2,1)S(1)}, u32[]{:S(2)}, u32[]{:S(2)}) %collective-permute-start.3) | collective-permute-done | bytes 524320 | tf_op jit(solution)/shard_map/ppermute | solution.py:31
  24.9 12.9 %collective-permute-done.4 = bf16[8,128,256]{2,1,0:T(8,128)(2,1)S(1)} collective-permute-done((bf16[8,128,256]{2,1,0:T(8,128)(2,1)S(1)}, bf16[8,128,256]{2,1,0:T(8,128)(2,1)S(1)}, u32[]{:S(2)}, u32[]{:S(2)}) %collective-permute-start.4) | collective-permute-done | bytes 524320 | tf_op jit(solution)/shard_map/ppermute | solution.py:31
  37.8 0.9 shard_map.100
  39.5 5.2 %collective-permute-done.6.rest_0_ = bf16[256,256]{1,0:T(8,128)(2,1)S(1)} collective-permute-done((bf16[256,256]{1,0:T(8,128)(2,1)S(1)}, bf16[256,256]{1,0:T(8,128)(2,1)S(1)}, u32[]{:S(2)}, u32[]{:S(2)}) %collective-permute-start.6) | collective-permute-done | bytes 131104 | tf_op jit(solution)/shard_map/ppermute | solution.py:31
  45.5 2.0 %collective-permute-start.8 = (bf16[64,256]{1,0:T(8,128)(2,1)S(1)}, bf16[64,256]{1,0:T(8,128)(2,1)S(1)}, u32[]{:S(2)}, u32[]{:S(2)}) collective-permute-start(bf16[64,256]{1,0:T(8,128)(2,1)S(1)} %get-tuple-element.27), channel_id=1, source_target_pairs={{0,8},{4,12},{8,0},{12,4},{1,9},{5,13},{9,1},{13,5},{2,10},{6,14},... | collective-permute-start | bytes 98312 | tf_op jit(solution)/shard_map/ppermute | solution.py:31
  47.6 13.5 %collective-permute-done.7.rest_0_ = bf16[64,256]{1,0:T(8,128)(2,1)S(1)} collective-permute-done((bf16[64,256]{1,0:T(8,128)(2,1)S(1)}, bf16[64,256]{1,0:T(8,128)(2,1)S(1)}, u32[]{:S(2)}, u32[]{:S(2)}) %collective-permute-start.7) | collective-permute-done | bytes 32800 | tf_op jit(solution)/shard_map/ppermute | solution.py:31
  61.0 2.0 %collective-permute-start.9 = (bf16[64,256]{1,0:T(8,128)(2,1)S(1)}, bf16[64,256]{1,0:T(8,128)(2,1)S(1)}, u32[]{:S(2)}, u32[]{:S(2)}) collective-permute-start(bf16[64,256]{1,0:T(8,128)(2,1)S(1)} %get-tuple-element.28), channel_id=1, source_target_pairs={{0,12},{4,0},{8,4},{12,8},{1,13},{5,1},{9,5},{13,9},{2,14},{6,2},{... | collective-permute-start | bytes 98312 | tf_op jit(solution)/shard_map/ppermute | solution.py:31
  63.0 2.0 %collective-permute-done.9.rest_2_ = bf16[64,256]{1,0:T(8,128)(2,1)S(1)} collective-permute-done((bf16[64,256]{1,0:T(8,128)(2,1)S(1)}, bf16[64,256]{1,0:T(8,128)(2,1)S(1)}, u32[]{:S(2)}, u32[]{:S(2)}) %collective-permute-start.9) | collective-permute-done | bytes 32800 | tf_op jit(solution)/shard_map/ppermute | solution.py:31
  65.7 3.9 %collective-permute-start.11 = (bf16[64,256]{1,0:T(8,128)(2,1)S(1)}, bf16[64,256]{1,0:T(8,128)(2,1)S(1)}, u32[]{:S(2)}, u32[]{:S(2)}) collective-permute-start(bf16[64,256]{1,0:T(8,128)(2,1)S(1)} %shard_map.103.refs_0_), channel_id=1, source_target_pairs={{0,8},{4,12},{8,0},{12,4},{1,9},{5,13},{9,1},{13,5},{2,10},{6,14},... | collective-permute-start | bytes 98312 | tf_op jit(solution)/shard_map/ppermute | solution.py:31
  69.7 1.4 %collective-permute-done.10.refs_1_ = bf16[64,256]{1,0:T(8,128)(2,1)S(1)} collective-permute-done((bf16[64,256]{1,0:T(8,128)(2,1)S(1)}, bf16[64,256]{1,0:T(8,128)(2,1)S(1)}, u32[]{:S(2)}, u32[]{:S(2)}) %collective-permute-start.10) | collective-permute-done | bytes 32800 | tf_op jit(solution)/shard_map/ppermute | solution.py:31
  71.1 1.9 %collective-permute-start.12 = (bf16[64,256]{1,0:T(8,128)(2,1)S(1)}, bf16[64,256]{1,0:T(8,128)(2,1)S(1)}, u32[]{:S(2)}, u32[]{:S(2)}) collective-permute-start(bf16[64,256]{1,0:T(8,128)(2,1)S(1)} %shard_map.103.refs_0_), channel_id=1, source_target_pairs={{0,12},{4,0},{8,4},{12,8},{1,13},{5,1},{9,5},{13,9},{2,14},{6,2},{... | collective-permute-start | bytes 98312 | tf_op jit(solution)/shard_map/ppermute | solution.py:31
  73.0 2.0 %collective-permute-done.12.refs_3_ = bf16[64,256]{1,0:T(8,128)(2,1)S(1)} collective-permute-done((bf16[64,256]{1,0:T(8,128)(2,1)S(1)}, bf16[64,256]{1,0:T(8,128)(2,1)S(1)}, u32[]{:S(2)}, u32[]{:S(2)}) %collective-permute-start.12) | collective-permute-done | bytes 32800 | tf_op jit(solution)/shard_map/ppermute | solution.py:31
  75.9 1.9 %shard_map.95.start = f32[8,128,256]{2,1,0:T(8,128)S(1)} custom-call(s32[1,1]{1,0:T(1,128)S(6)} %copy.10.counts, s32[1,36]{1,0:T(1,128)S(1)} %copy-done.7, s32[1,36]{1,0:T(1,128)S(1)} %copy-done.9, bf16[36,128,128]{2,1,0:T(8,128)(2,1)S(1)} %bitcast.15, bf16[8,128,256]{2,1,0:T(8,128)(2,1)S(1)} %bitcast.26, bf16[8,128,256]{2,1,0:T(8,128)(2,1)S(1)} %bitcast.24), custom_call_target="tpu_custom_call" | custom-call | flops 100663296 | bytes 1048576 | tf_op jit(solution)/shard_map/pallas_call | solution.py:18
  77.8 2.3 %collective-permute-done.13.refs_1_ = bf16[256,256]{1,0:T(8,128)(2,1)S(1)} collective-permute-done((bf16[256,256]{1,0:T(8,128)(2,1)S(1)}, bf16[256,256]{1,0:T(8,128)(2,1)S(1)}, u32[]{:S(2)}, u32[]{:S(2)}) %collective-permute-start.13) | collective-permute-done | bytes 131104 | tf_op jit(solution)/shard_map/ppermute | solution.py:31
  80.1 0.8 shard_map.105
  80.9 1.7 %shard_map.96.start = f32[8,128,256]{2,1,0:T(8,128)S(1)} custom-call(s32[1,1]{1,0:T(1,128)S(6)} %copy.10.counts, s32[1,36]{1,0:T(1,128)S(1)} %copy-done.7, s32[1,36]{1,0:T(1,128)S(1)} %copy-done.9, bf16[36,128,128]{2,1,0:T(8,128)(2,1)S(1)} %bitcast.16, bf16[8,128,256]{2,1,0:T(8,128)(2,1)S(1)} %bitcast.29, f32[8,128,256]{2,1,0:T(8,128)S(1)} %shard_map.95.start), custom_call_target="tpu_custom_call" | custom-call | flops 100663296 | bytes 1048576 | tf_op jit(solution)/shard_map/pallas_call | solution.py:18
  82.6 2.5 %shard_map.97 = bf16[8,128,256]{2,1,0:T(8,128)(2,1)} custom-call(s32[1,1]{1,0:T(1,128)S(6)} %copy.10.counts, s32[1,36]{1,0:T(1,128)S(1)} %copy-done.7, s32[1,36]{1,0:T(1,128)S(1)} %copy-done.9, bf16[36,128,128]{2,1,0:T(8,128)(2,1)S(1)} %bitcast.17, bf16[8,128,256]{2,1,0:T(8,128)(2,1)S(1)} %bitcast.25, f32[8,128,256]{2,1,0:T(8,128)S(1)} %shard_map.96.start), custom_call_target="tpu_custom_call" | custom-call | flops 100663296 | bytes 1048576 | tf_op jit(solution)/shard_map/pallas_call | solution.py:18
  85.1 0.9 %shard_map.101 = bf16[1024,256]{1,0:T(8,128)(2,1)} custom-call(f32[1024,256]{1,0:T(8,128)S(1)} %get-tuple-element.21.gsum, bf16[1024,256]{1,0:T(8,128)(2,1)S(1)} %collective-permute-done.5.arrived), custom_call_target="tpu_custom_call" | custom-call | bytes 2097152 | tf_op jit(solution)/shard_map/pallas_call | solution.py:18
  (36 shorter events, 5.9 us)
Async XLA Ops:
  0.6 14.0 %collective-permute-start = (bf16[1024,256]{1,0:T(8,128)(2,1)}, bf16[1024,256]{1,0:T(8,128)(2,1)S(1)}, u32[]{:S(2)}, u32[]{:S(2)}) collective-permute-start(bf16[1024,256]{1,0:T(8,128)(2,1)} %bitcast.22), channel_id=1, source_target_pairs={{0,1},{1,0},{2,3},{3,2},{4,5},{5,4},{6,7},{7,6},{8,9},{9,8},{10,11... | collective-permute-start | bytes 1572872 | tf_op jit(solution)/shard_map/ppermute | solution.py:31
  1.8 1.3 %copy-start = (bf16[1,36,128,128]{3,2,1,0:T(8,128)(2,1)S(1)}, bf16[1,36,128,128]{3,2,1,0:T(8,128)(2,1)}, u32[]{:S(2)}) copy-start(bf16[1,36,128,128]{3,2,1,0:T(8,128)(2,1)} %param.9) | copy-start | bytes 3538948
  3.1 1.0 %copy-start.2 = (bf16[1,1024,256]{2,1,0:T(8,128)(2,1)S(1)}, bf16[1,1024,256]{2,1,0:T(8,128)(2,1)}, u32[]{:S(2)}) copy-start(bf16[1,1024,256]{2,1,0:T(8,128)(2,1)} %param.13) | copy-start | bytes 1572868
  4.1 0.7 copy-start.6
  4.8 0.7 copy-start.8
  8.4 16.4 %collective-permute-start.3 = (bf16[8,128,256]{2,1,0:T(8,128)(2,1)S(1)}, bf16[8,128,256]{2,1,0:T(8,128)(2,1)S(1)}, u32[]{:S(2)}, u32[]{:S(2)}) collective-permute-start(bf16[8,128,256]{2,1,0:T(8,128)(2,1)S(1)} %get-tuple-element.17), channel_id=1, source_target_pairs={{0,12},{4,0},{8,4},{12,8},{1,13},{5,1},{9,5},{13,9},{2,14},{6,2},{... | collective-permute-start | bytes 1572872 | tf_op jit(solution)/shard_map/ppermute | solution.py:31
  12.6 2.1 %copy-start.4 = (bf16[1,1024,256]{2,1,0:T(8,128)(2,1)S(1)}, bf16[1,1024,256]{2,1,0:T(8,128)(2,1)}, u32[]{:S(2)}) copy-start(bf16[1,1024,256]{2,1,0:T(8,128)(2,1)} %param.7) | copy-start | bytes 1572868
  12.6 2.1 %copy-start.5 = (bf16[512,256]{1,0:T(8,128)(2,1)S(1)}, bf16[512,256]{1,0:T(8,128)(2,1)}, u32[]{:S(2)}) copy-start(bf16[512,256]{1,0:T(8,128)(2,1)} %weight.3) | copy-start | bytes 786436
  12.6 25.2 %collective-permute-start.4 = (bf16[8,128,256]{2,1,0:T(8,128)(2,1)S(1)}, bf16[8,128,256]{2,1,0:T(8,128)(2,1)S(1)}, u32[]{:S(2)}, u32[]{:S(2)}) collective-permute-start(bf16[8,128,256]{2,1,0:T(8,128)(2,1)S(1)} %get-tuple-element.18), channel_id=1, source_target_pairs={{0,4},{4,8},{8,12},{12,0},{1,5},{5,9},{9,13},{13,1},{2,6},{6,10},{... | collective-permute-start | bytes 1572872 | tf_op jit(solution)/shard_map/ppermute | solution.py:31
  14.6 23.1 %copy-start.3 = (bf16[1,1024,256]{2,1,0:T(8,128)(2,1)S(1)}, bf16[1,1024,256]{2,1,0:T(8,128)(2,1)}, u32[]{:S(2)}) copy-start(bf16[1,1024,256]{2,1,0:T(8,128)(2,1)} %param.13) | copy-start | bytes 1572868
  15.4 67.2 %collective-permute-start.1 = (bf16[1024,256]{1,0:T(8,128)(2,1)S(1)}, bf16[1024,256]{1,0:T(8,128)(2,1)S(1)}, u32[]{:S(2)}, u32[]{:S(2)}) collective-permute-start(bf16[1024,256]{1,0:T(8,128)(2,1)S(1)} %get-tuple-element.16), channel_id=1, source_target_pairs={{0,12},{4,0},{8,4},{12,8},{1,13},{5,1},{9,5},{13,9},{2,14},{6,2},{... | collective-permute-start | bytes 1572872 | tf_op jit(solution)/shard_map/ppermute | solution.py:31
  18.5 62.5 %collective-permute-start.2 = (bf16[1024,256]{1,0:T(8,128)(2,1)S(1)}, bf16[1024,256]{1,0:T(8,128)(2,1)S(1)}, u32[]{:S(2)}, u32[]{:S(2)}) collective-permute-start(bf16[1024,256]{1,0:T(8,128)(2,1)S(1)} %get-tuple-element.16), channel_id=1, source_target_pairs={{0,4},{4,8},{8,12},{12,0},{1,5},{5,9},{9,13},{13,1},{2,6},{6,10},{... | collective-permute-start | bytes 1572872 | tf_op jit(solution)/shard_map/ppermute | solution.py:31
  37.8 38.1 %copy-start.1 = (bf16[1,36,128,128]{3,2,1,0:T(8,128)(2,1)S(1)}, bf16[1,36,128,128]{3,2,1,0:T(8,128)(2,1)}, u32[]{:S(2)}) copy-start(bf16[1,36,128,128]{3,2,1,0:T(8,128)(2,1)} %param.9) | copy-start | bytes 3538948
  37.8 38.1 %copy-start.7 = (s32[1,36]{1,0:T(1,128)S(1)}, s32[1,36]{1,0:T(1,128)}, u32[]{:S(2)}) copy-start(s32[1,36]{1,0:T(1,128)} %target.9) | copy-start | bytes 436
  37.8 38.1 %copy-start.9 = (s32[1,36]{1,0:T(1,128)S(1)}, s32[1,36]{1,0:T(1,128)}, u32[]{:S(2)}) copy-start(s32[1,36]{1,0:T(1,128)} %source.9) | copy-start | bytes 436
  38.7 46.4 %collective-permute-start.5 = (bf16[1024,256]{1,0:T(8,128)(2,1)S(1)}, bf16[1024,256]{1,0:T(8,128)(2,1)S(1)}, u32[]{:S(2)}, u32[]{:S(2)}) collective-permute-start(bf16[1024,256]{1,0:T(8,128)(2,1)S(1)} %get-tuple-element.22), channel_id=1, source_target_pairs={{0,1},{1,0},{2,3},{3,2},{4,5},{5,4},{6,7},{7,6},{8,9},{9,8},{10,11... | collective-permute-start | bytes 1572872 | tf_op jit(solution)/shard_map/ppermute | solution.py:31
  38.7 5.9 %collective-permute-start.6 = (bf16[256,256]{1,0:T(8,128)(2,1)S(1)}, bf16[256,256]{1,0:T(8,128)(2,1)S(1)}, u32[]{:S(2)}, u32[]{:S(2)}) collective-permute-start(bf16[256,256]{1,0:T(8,128)(2,1)S(1)} %get-tuple-element.24), channel_id=1, source_target_pairs={{0,2},{2,0},{1,3},{3,1},{4,6},{6,4},{5,7},{7,5},{8,10},{10,8},{9,1... | collective-permute-start | bytes 393224 | tf_op jit(solution)/shard_map/ppermute | solution.py:31
  44.7 16.3 %collective-permute-start.7 = (bf16[64,256]{1,0:T(8,128)(2,1)S(1)}, bf16[64,256]{1,0:T(8,128)(2,1)S(1)}, u32[]{:S(2)}, u32[]{:S(2)}) collective-permute-start(bf16[64,256]{1,0:T(8,128)(2,1)S(1)} %get-tuple-element.26), channel_id=1, source_target_pairs={{0,4},{4,8},{8,12},{12,0},{1,5},{5,9},{9,13},{13,1},{2,6},{6,10},{... | collective-permute-start | bytes 98312 | tf_op jit(solution)/shard_map/ppermute | solution.py:31
  45.5 17.4 %collective-permute-start.8 = (bf16[64,256]{1,0:T(8,128)(2,1)S(1)}, bf16[64,256]{1,0:T(8,128)(2,1)S(1)}, u32[]{:S(2)}, u32[]{:S(2)}) collective-permute-start(bf16[64,256]{1,0:T(8,128)(2,1)S(1)} %get-tuple-element.27), channel_id=1, source_target_pairs={{0,8},{4,12},{8,0},{12,4},{1,9},{5,13},{9,1},{13,5},{2,10},{6,14},... | collective-permute-start | bytes 98312 | tf_op jit(solution)/shard_map/ppermute | solution.py:31
  61.0 3.9 %collective-permute-start.9 = (bf16[64,256]{1,0:T(8,128)(2,1)S(1)}, bf16[64,256]{1,0:T(8,128)(2,1)S(1)}, u32[]{:S(2)}, u32[]{:S(2)}) collective-permute-start(bf16[64,256]{1,0:T(8,128)(2,1)S(1)} %get-tuple-element.28), channel_id=1, source_target_pairs={{0,12},{4,0},{8,4},{12,8},{1,13},{5,1},{9,5},{13,9},{2,14},{6,2},{... | collective-permute-start | bytes 98312 | tf_op jit(solution)/shard_map/ppermute | solution.py:31
  65.0 6.2 %collective-permute-start.10 = (bf16[64,256]{1,0:T(8,128)(2,1)S(1)}, bf16[64,256]{1,0:T(8,128)(2,1)S(1)}, u32[]{:S(2)}, u32[]{:S(2)}) collective-permute-start(bf16[64,256]{1,0:T(8,128)(2,1)S(1)} %shard_map.103.refs_0_), channel_id=1, source_target_pairs={{0,4},{4,8},{8,12},{12,0},{1,5},{5,9},{9,13},{13,1},{2,6},{6,10},{... | collective-permute-start | bytes 98312 | tf_op jit(solution)/shard_map/ppermute | solution.py:31
  65.7 7.3 %collective-permute-start.11 = (bf16[64,256]{1,0:T(8,128)(2,1)S(1)}, bf16[64,256]{1,0:T(8,128)(2,1)S(1)}, u32[]{:S(2)}, u32[]{:S(2)}) collective-permute-start(bf16[64,256]{1,0:T(8,128)(2,1)S(1)} %shard_map.103.refs_0_), channel_id=1, source_target_pairs={{0,8},{4,12},{8,0},{12,4},{1,9},{5,13},{9,1},{13,5},{2,10},{6,14},... | collective-permute-start | bytes 98312 | tf_op jit(solution)/shard_map/ppermute | solution.py:31
  71.1 3.9 %collective-permute-start.12 = (bf16[64,256]{1,0:T(8,128)(2,1)S(1)}, bf16[64,256]{1,0:T(8,128)(2,1)S(1)}, u32[]{:S(2)}, u32[]{:S(2)}) collective-permute-start(bf16[64,256]{1,0:T(8,128)(2,1)S(1)} %shard_map.103.refs_0_), channel_id=1, source_target_pairs={{0,12},{4,0},{8,4},{12,8},{1,13},{5,1},{9,5},{13,9},{2,14},{6,2},{... | collective-permute-start | bytes 98312 | tf_op jit(solution)/shard_map/ppermute | solution.py:31
  75.1 5.0 %collective-permute-start.13 = (bf16[256,256]{1,0:T(8,128)(2,1)S(1)}, bf16[256,256]{1,0:T(8,128)(2,1)S(1)}, u32[]{:S(2)}, u32[]{:S(2)}) collective-permute-start(bf16[256,256]{1,0:T(8,128)(2,1)S(1)} %shard_map.104.refs_0_), channel_id=1, source_target_pairs={{0,2},{2,0},{1,3},{3,1},{4,6},{6,4},{5,7},{7,5},{8,10},{10,8},{9,1... | collective-permute-start | bytes 393224 | tf_op jit(solution)/shard_map/ppermute | solution.py:31

commit v2 on v1

v2 whole, which is shorter than its diff:
```python
import functools

import jax
import jax.numpy as jnp
from jax import lax
from jax.experimental import pallas as pl
from jax.experimental.pallas import tpu as pltpu
from jax.sharding import PartitionSpec as P

F32 = jnp.float32
BF16 = jnp.bfloat16
UNROLL = 4
VMEM = pl.BlockSpec(memory_space=pltpu.VMEM)
SMEM = pl.BlockSpec(memory_space=pltpu.SMEM)
HBM = pl.BlockSpec(memory_space=pltpu.HBM)


def call(body, ins, outs, scratch=(), flops=0, nbytes=0, space=None):
    return pl.pallas_call(
        body,
        in_specs=[space or (SMEM if x.dtype == jnp.int32 else VMEM) for x in ins],
        out_shape=[jax.ShapeDtypeStruct(s, d) for s, d in outs],
        out_specs=[VMEM for _ in outs],
        scratch_shapes=list(scratch),
        cost_estimate=pl.CostEstimate(flops=flops, bytes_accessed=nbytes, transcendentals=0),
        compiler_params=pltpu.CompilerParams(vmem_limit_bytes=32 * 1024 * 1024),
    )(*ins)


def shift(value, axis, steps):
    count = lax.axis_size(axis)
    return lax.ppermute(value, axis, [(i, (i + steps) % count) for i in range(count)])


def pick(listed, count, source, low, high):
    slots = source.shape[1]

    def step(k, found):
        listed[found] = k
        s = source[0, k]
        inside = (k < count) & (s >= low) & (s < high)
        return found + inside.astype(jnp.int32)

    found = lax.fori_loop(0, slots, step, jnp.int32(0))
    for j in range(UNROLL):
        listed[found + j] = 0
    return found


def over_tiles(listed, found, step):
    def some(i, carry):
        for j in range(UNROLL):
            at = i * UNROLL + j
            step(listed[at], at < found)
        return carry

    lax.fori_loop(0, (found + UNROLL - 1) // UNROLL, some, 0)


def back_body(ranges, nblocks, counts_hbm, target_hbm, source_hbm, tiles_hbm, grads_hbm, *rest):
    n = len(ranges)
    outs = rest[:n]
    acc, listed, counts, target, source, tiles, grads, sems = rest[n:]
    copies = [
        pltpu.make_async_copy(there, here, sems.at[i])
        for i, (there, here) in enumerate(
            [
                (counts_hbm, counts),
                (source_hbm, source),
                (target_hbm, target),
                (grads_hbm, grads),
                (tiles_hbm, tiles),
            ]
        )
    ]
    for copy in copies:
        copy.start()
    acc[...] = jnp.zeros_like(acc)
    for copy in copies:
        copy.wait()
    for low, out in zip(ranges, outs):
        if low != ranges[0]:
            acc[...] = jnp.zeros_like(acc)
        found = pick(listed, counts[0, 0], source, low, low + nblocks)

        def step(k, valid):
            at = jnp.where(valid, source[0, k] - low, nblocks)
            acc[at] += lax.dot_general(
                tiles[k], grads[target[0, k]], (((0,), (0,)), ((), ())), preferred_element_type=F32
            )

        over_tiles(listed, found, step)
        for b in range(nblocks):
            out[b] = acc[b].astype(out.dtype)


def triplet_body(lows, nblocks, counts, target, source, tiles, *rest):
    n = len(lows)
    rows, start, out, acc, listed = rest[:n], *rest[n:]
    for b in range(nblocks):
        acc[b] = start[b].astype(F32)
    for low, piece in zip(lows, rows):
        found = pick(listed, counts[0, 0], source, low, low + piece.shape[0])

        def step(k, valid):
            at = jnp.where(valid, target[0, k], nblocks)
            s = jnp.where(valid, source[0, k] - low, 0)
            acc[at] += jnp.dot(tiles[k], piece[s], preferred_element_type=F32)

        over_tiles(listed, found, step)
    for b in range(nblocks):
        out[b] = acc[b].astype(out.dtype)


def preact_body(step, mine, theirs, weight, act, factor, flipped):
    rows, chans = mine.shape
    core = lax.axis_index("tensor")
    own = pl.ds(pl.multiple_of(core * chans, chans), chans)
    other = pl.ds(pl.multiple_of((1 - core) * chans, chans), chans)
    for r in range(0, rows, step):
        at = pl.ds(r, step)
        pre = jnp.dot(mine[at], weight[own], preferred_element_type=F32) + jnp.dot(
            theirs[at], weight[other], preferred_element_type=F32
        )
        sig = 1.0 / (1.0 + jnp.exp(-pre))
        act[at] = (pre * sig).astype(BF16)
        factor[at] = sig * (1.0 + pre * (1.0 - sig))
        flipped[own, at] = mine[at].T
        flipped[other, at] = theirs[at].T


def partners():
    return [(f, d) for f in (1, 0) for d in range(lax.axis_size("dp")) if (f, d) != (0, 0)]


def to_partner(value, flip, steps):
    nz, ndp = lax.axis_size("graph"), lax.axis_size("dp")
    pairs = [
        (z * ndp + d, (z ^ flip) * ndp + (d + steps) % ndp) for z in range(nz) for d in range(ndp)
    ]
    return lax.ppermute(value, ("graph", "dp"), pairs)


def place(flip, steps, size):
    ndp = lax.axis_size("dp")
    d = lax.rem(lax.axis_index("dp") + steps + ndp, ndp)
    b = lax.rem(lax.axis_index("graph") + flip, 2)
    return pl.ds(pl.multiple_of((d * 2 + b) * size, size), size)


def slope_body(step, back, from_next, from_prev, factor, grads, weight, flipped, *rest):
    to_core, gsum, keep = rest[:3]
    others = partners()
    sends = rest[3 : 3 + len(others)]
    slope, part = rest[3 + len(others) :]
    rows, chans = grads.shape
    core = lax.axis_index("tensor")
    own = pl.ds(pl.multiple_of(core * chans, chans), chans)
    other = pl.ds(pl.multiple_of((1 - core) * chans, chans), chans)
    last = (((1,), (1,)), ((), ()))
    for r in range(0, rows, step):
        at = pl.ds(r, step)
        total = back[at] + from_next[at].astype(F32) + from_prev[at].astype(F32)
        piece = (total * factor[at]).astype(BF16)
        slope[at] = piece
        to_core[at] = lax.dot_general(piece, weight[other], last, preferred_element_type=F32).astype(BF16)
        gsum[at] = grads[at].astype(F32) + lax.dot_general(
            piece, weight[own], last, preferred_element_type=F32
        )
    part[...] = jnp.dot(flipped[...], slope[...], preferred_element_type=F32)
    size = keep.shape[0]
    keep[...] = part[place(0, 0, size)]
    for (flip, steps), send in zip(others, sends):
        send[...] = part[place(flip, steps, size)].astype(BF16)


def grads_body(gsum, arrived, out):
    out[...] = (gsum[...] + arrived[...].astype(F32)).astype(BF16)


def total_body(scale, *refs):
    total = refs[0][...].astype(F32)
    for ref in refs[1:-1]:
        total = total + ref[...].astype(F32)
    refs[-1][...] = (total * scale).astype(BF16)


def gather_body(mine, *rest):
    out = rest[-1]
    size = mine.shape[0]
    out[place(0, 0, size)] = mine[...].astype(F32)
    for (flip, steps), ref in zip(partners(), rest):
        out[place(flip, -steps, size)] = ref[...].astype(F32)


def bits(nz):
    return [1 << i for i in range(1, nz.bit_length() - 1)]


def shards(edges_in, weight, basis_tiles, target_blocks, source_blocks, counts, grad_out):
    rows, chans = edges_in.shape[1], edges_in.shape[2]
    tile = basis_tiles.shape[2]
    nblocks = rows // tile
    slots = basis_tiles.shape[1]
    depth = weight.shape[0]
    ndp, nz = lax.axis_size("dp"), lax.axis_size("graph")
    mine, grads, tiles = edges_in[0], grad_out[0], basis_tiles[0]
    blocks = (nblocks, tile, chans)
    flat = (rows, chans)
    index = [counts, target_blocks, source_blocks, tiles]
    work = [pltpu.VMEM((nblocks + 1, tile, chans), F32), pltpu.SMEM((slots + UNROLL,), jnp.int32)]
    unit = 2 * tile * tile * chans * slots // 3

    half = nblocks // 2
    theirs = shift(mine, "tensor", 1)

    def back_terms(ranges, kinds):
        return call(
            functools.partial(back_body, ranges, nblocks),
            [*index, grads.reshape(blocks)],
            [(blocks, kind) for kind in kinds],
            work
            + [pltpu.SMEM(x.shape, jnp.int32) for x in index[:3]]
            + [pltpu.VMEM(tiles.shape, BF16), pltpu.VMEM(blocks, BF16), pltpu.SemaphoreType.DMA((5,))],
            flops=len(ranges) * unit,
            nbytes=4 * rows * chans,
            space=HBM,
        )

    to_prev, to_next = back_terms((0, 2 * nblocks), (BF16, BF16))
    from_next = shift(to_prev, "graph", -1)
    from_prev = shift(to_next, "graph", 1)
    (back,) = back_terms((nblocks,), (F32,))
    act, factor, flipped = call(
        functools.partial(preact_body, 256),
        [mine, theirs, weight],
        [(flat, BF16), (flat, F32), ((depth, rows), BF16)],
        flops=2 * rows * depth * chans,
        nbytes=8 * rows * chans,
    )
    act = act.reshape(blocks)
    low_act, high_act = act[:half], act[half:]

    def triplet(lows, pieces, start, kind):
        (acc,) = call(
            functools.partial(triplet_body, lows, nblocks),
            [*index, *pieces, start],
            [(blocks, kind)],
            work,
            flops=unit,
            nbytes=4 * rows * chans,
        )
        return acc

    prev_low = shift(low_act, "graph", 1)
    others = partners()
    size = depth // (len(others) + 1)
    to_core, gsum, keep, *sends = call(
        functools.partial(slope_body, 256),
        [back.reshape(flat), from_next.reshape(flat), from_prev.reshape(flat), factor, grads, weight, flipped],
        [(flat, BF16), (flat, F32), ((size, chans), F32)] + [((size, chans), BF16)] * len(others),
        [pltpu.VMEM(flat, BF16), pltpu.VMEM((depth, chans), F32)],
        flops=4 * rows * depth * chans,
        nbytes=8 * rows * chans,
    )
    arrived = [to_partner(s, *at) for s, at in zip(sends, others)]
    high_now, _ = lax.optimization_barrier((high_act, keep))
    prev_high = shift(high_now, "graph", 1)
    summed = shift(to_core, "tensor", 1)
    (grad_edges,) = call(grads_body, [gsum, summed], [(flat, BF16)], nbytes=8 * rows * chans)

    def add_up(scale, parts):
        return call(functools.partial(total_body, scale), parts, [((size, chans), BF16)])[0]

    scale = float(1.0 / (ndp * edges_in.shape[0] * nz * rows) ** 0.5)
    stages = bits(nz)
    total = add_up(1.0 if stages else scale, [keep, *arrived])
    low_now, _ = lax.optimization_barrier((low_act, total))
    next_low = shift(low_now, "graph", -1)
    for i, bit in enumerate(stages):
        swapped = lax.ppermute(total, "graph", [(z, z ^ bit) for z in range(nz)])
        total = add_up(scale if i + 1 == len(stages) else 1.0, [total, swapped])
    high_now, _ = lax.optimization_barrier((high_act, total))
    next_high = shift(high_now, "graph", -1)
    arrived = [to_partner(total, *at) for at in others]
    (grad_weight,) = call(gather_body, [total, *arrived], [((depth, chans), F32)])

    acc = triplet((nblocks, 0, half), (act, prev_low, prev_high), mine.reshape(blocks), F32)
    acc = triplet((2 * nblocks,), (next_low,), acc, F32)
    edges_out = triplet((2 * nblocks + half,), (next_high,), acc, BF16)
    return edges_out.reshape(1, rows, chans), grad_edges[None], grad_weight


def solution(mesh):
    placed = (
        P(("parts", "dp"), "graph", "tensor"),
        P(None, "tensor"),
        P(("parts", "dp"), "graph", None, None),
        P(("parts", "dp"), "graph"),
        P(("parts", "dp"), "graph"),
        P(("parts", "dp"), "graph"),
        P(("parts", "dp"), "graph", "tensor"),
    )
    return jax.shard_map(
        shards,
        mesh=mesh,
        in_specs=placed,
        out_specs=(
            P(("parts", "dp"), "graph", "tensor"),
            P(("parts", "dp"), "graph", "tensor"),
            P("parts", "tensor"),
        ),
        check_vma=False,
    )
```

time: 85.6 us -> 82.8 us (0.967)
  starting transfers between devices: 20.8 us -> 15.7 us
  waiting for transfers between devices: 45.6 us -> 48.7 us
  Pallas kernels: 14.5 us -> 13.1 us
    ppermute x0 -> x7, waiting for transfers between devices: none -> 20.1 us  [the longest x6 15.1 us: to_partner(): return lax.ppermute(value, ('graph', 'dp'), pairs)]
    ppermute x14 -> x8, waiting for transfers between devices: 45.6 us -> 28.5 us  [shift(): lax.ppermute(value, axis, [(i, (i + steps) % count) for i in range(count)])]
    ppermute x14 -> x8, starting transfers between devices: 20.8 us -> 7.95 us  [shift(): lax.ppermute(value, axis, [(i, (i + steps) % count) for i in range(count)])]
    ppermute x0 -> x7, starting transfers between devices: none -> 7.78 us  [the longest x6 7.1 us: to_partner(): return lax.ppermute(value, ('graph', 'dp'), pairs)]
    pallas_call x12 -> x11, Pallas kernels: 14.5 us -> 13.1 us  [call(): pl.pallas_call(body, in_specs=[space or (SMEM if x.dtype == jnp.int32 els...]
  transfers between devices with their start and end apart: 14 -> 15, of which waited for: 8 -> 12; matrix products, arithmetic and copies ran while one was open for 0% -> 0% of each run, Pallas kernels for 16% -> 14%
where the time goes in v2:
time: 82.8 us; the launch traced here: 82.6 us
  waiting for transfers between devices  48.7 us (59%)
  starting transfers between devices  15.7 us (19%)
  Pallas kernels  13.1 us (16%)
  local copies, waits for them, and re-layouts  3.68 us (4%)
  between operations  1.42 us (2%)
    ppermute x8, waiting for transfers between devices, shift(): lax.ppermute(value, axis, [(i, (i + steps) % count) for i in range(count)])  28.5 us
    ppermute x6, waiting for transfers between devices, to_partner(): return lax.ppermute(value, ('graph', 'dp'), pairs)  15.1 us
    pallas_call x11, Pallas kernels, call(): pl.pallas_call(body, in_specs=[space or (SMEM if x.dtype == jnp.int32 els...  13.1 us
    ppermute x8, starting transfers between devices, shift(): lax.ppermute(value, axis, [(i, (i + steps) % count) for i in range(count)])  7.95 us
    ppermute x6, starting transfers between devices, to_partner(): return lax.ppermute(value, ('graph', 'dp'), pairs)  7.1 us
    ppermute x1, waiting for transfers between devices, shards(): swapped = lax.ppermute(total, 'graph', [(z, z ^ bit) for z in range(nz)])  5.07 us
    unnamed x20, local copies, waits for them, and re-layouts  3.64 us
  transfers between devices with their start and end apart: 15, of which 12 were waited for; matrix products, arithmetic and copies ran while one was open for 0% of the time, Pallas kernels for 14%

profile of v2, /device:TPU:0, one launch (start us, length us, event | category | flops | bytes accessed | tf_op | source)
XLA Modules:
  0.0 82.6 jit_solution(15473444703431920625)
XLA Ops:
  1.8 1.3 %copy-done = bf16[1,36,128,128]{3,2,1,0:T(8,128)(2,1)S(1)} copy-done((bf16[1,36,128,128]{3,2,1,0:T(8,128)(2,1)S(1)}, bf16[1,36,128,128]{3,2,1,0:T(8,128)(2,1)}, u32[]{:S(2)}) %copy-start) | copy-done | bytes 1179672
  3.1 1.0 %copy-done.2 = bf16[1,1024,256]{2,1,0:T(8,128)(2,1)S(1)} copy-done((bf16[1,1024,256]{2,1,0:T(8,128)(2,1)S(1)}, bf16[1,1024,256]{2,1,0:T(8,128)(2,1)}, u32[]{:S(2)}) %copy-start.2) | copy-done | bytes 524312
  5.4 2.5 %shard_map.96 = (bf16[8,128,256]{2,1,0:T(8,128)(2,1)S(1)}, bf16[8,128,256]{2,1,0:T(8,128)(2,1)S(1)}) custom-call(s32[1,1]{1,0:T(1,128)S(6)} %copy.10.counts_hbm.counts, s32[1,36]{1,0:T(1,128)S(1)} %copy-done.6, s32[1,36]{1,0:T(1,128)S(1)} %copy-done.8, bf16[36,128,128]{2,1,0:T(8,128)(2,1)S(1)} %bitcast.13, bf16[8,128,256]{2,1,0:T(8,128)(2,1)S(1)} %bitcast.18), custom_call_target="tpu_custom_call" | custom-call | flops 201326592 | bytes 1048576 | tf_op jit(solution)/shard_map/pallas_call | solution.py:19
  7.9 5.5 %collective-permute-start.1 = (bf16[8,128,256]{2,1,0:T(8,128)(2,1)S(1)}, bf16[8,128,256]{2,1,0:T(8,128)(2,1)S(1)}, u32[]{:S(2)}, u32[]{:S(2)}) collective-permute-start(bf16[8,128,256]{2,1,0:T(8,128)(2,1)S(1)} %get-tuple-element.18), channel_id=1, source_target_pairs={{0,12},{4,0},{8,4},{12,8},{1,13},{5,1},{9,5},{13,9},{2,14},{6,2},{... | collective-permute-start | bytes 1572872 | tf_op jit(solution)/shard_map/ppermute | solution.py:32
  13.4 1.5 %shard_map.95 = f32[8,128,256]{2,1,0:T(8,128)S(1)} custom-call(s32[1,1]{1,0:T(1,128)S(6)} %copy.10.counts_hbm.counts, s32[1,36]{1,0:T(1,128)S(1)} %copy-done.6, s32[1,36]{1,0:T(1,128)S(1)} %copy-done.8, bf16[36,128,128]{2,1,0:T(8,128)(2,1)S(1)} %bitcast.14, bf16[8,128,256]{2,1,0:T(8,128)(2,1)S(1)} %bitcast.19), custom_call_target="tpu_custom_call" | custom-call | flops 100663296 | bytes 1048576 | tf_op jit(solution)/shard_map/pallas_call | solution.py:19
  15.7 10.0 %collective-permute-done.1 = bf16[8,128,256]{2,1,0:T(8,128)(2,1)S(1)} collective-permute-done((bf16[8,128,256]{2,1,0:T(8,128)(2,1)S(1)}, bf16[8,128,256]{2,1,0:T(8,128)(2,1)S(1)}, u32[]{:S(2)}, u32[]{:S(2)}) %collective-permute-start.1) | collective-permute-done | bytes 524320 | tf_op jit(solution)/shard_map/ppermute | solution.py:32
  25.6 11.5 %collective-permute-done.2 = bf16[8,128,256]{2,1,0:T(8,128)(2,1)S(1)} collective-permute-done((bf16[8,128,256]{2,1,0:T(8,128)(2,1)S(1)}, bf16[8,128,256]{2,1,0:T(8,128)(2,1)S(1)}, u32[]{:S(2)}, u32[]{:S(2)}) %collective-permute-start.2) | collective-permute-done | bytes 524320 | tf_op jit(solution)/shard_map/ppermute | solution.py:32
  38.0 1.9 %collective-permute-start.3 = (bf16[128,256]{1,0:T(8,128)(2,1)S(1)}, bf16[128,256]{1,0:T(8,128)(2,1)S(1)}, u32[]{:S(2)}, u32[]{:S(2)}) collective-permute-start(bf16[128,256]{1,0:T(8,128)(2,1)S(1)} %get-tuple-element.23), channel_id=1, source_target_pairs={{0,4},{2,6},{4,0},{6,2},{8,12},{10,14},{12,8},{14,10},{1,5},{3,7},... | collective-permute-start | bytes 196616 | tf_op jit(solution)/shard_map/ppermute | solution.py:141
  39.9 1.3 %collective-permute-start.4 = (bf16[128,256]{1,0:T(8,128)(2,1)S(1)}, bf16[128,256]{1,0:T(8,128)(2,1)S(1)}, u32[]{:S(2)}, u32[]{:S(2)}) collective-permute-start(bf16[128,256]{1,0:T(8,128)(2,1)S(1)} %get-tuple-element.24), channel_id=1, source_target_pairs={{0,6},{2,4},{4,2},{6,0},{8,14},{10,12},{12,10},{14,8},{1,7},{3,5},... | collective-permute-start | bytes 196616 | tf_op jit(solution)/shard_map/ppermute | solution.py:141
  41.6 1.4 %collective-permute-done.3.refs_1_ = bf16[128,256]{1,0:T(8,128)(2,1)S(1)} collective-permute-done((bf16[128,256]{1,0:T(8,128)(2,1)S(1)}, bf16[128,256]{1,0:T(8,128)(2,1)S(1)}, u32[]{:S(2)}, u32[]{:S(2)}) %collective-permute-start.3) | collective-permute-done | bytes 65568 | tf_op jit(solution)/shard_map/ppermute | solution.py:141
  43.0 2.1 %collective-permute-done.4.refs_2_ = bf16[128,256]{1,0:T(8,128)(2,1)S(1)} collective-permute-done((bf16[128,256]{1,0:T(8,128)(2,1)S(1)}, bf16[128,256]{1,0:T(8,128)(2,1)S(1)}, u32[]{:S(2)}, u32[]{:S(2)}) %collective-permute-start.4) | collective-permute-done | bytes 65568 | tf_op jit(solution)/shard_map/ppermute | solution.py:141
  46.5 5.1 %collective-permute-done.6.refs_1_ = bf16[128,256]{1,0:T(8,128)(2,1)S(1)} collective-permute-done((bf16[128,256]{1,0:T(8,128)(2,1)S(1)}, bf16[128,256]{1,0:T(8,128)(2,1)S(1)}, u32[]{:S(2)}, u32[]{:S(2)}) %collective-permute-start.6) | collective-permute-done | bytes 65568 | tf_op jit(solution)/shard_map/ppermute | solution.py:281
  51.6 1.4 %collective-permute-start.13 = (bf16[128,256]{1,0:T(8,128)(2,1)S(1)}, bf16[128,256]{1,0:T(8,128)(2,1)S(1)}, u32[]{:S(2)}, u32[]{:S(2)}) collective-permute-start(bf16[128,256]{1,0:T(8,128)(2,1)S(1)} %shard_map.99.mine), channel_id=1, source_target_pairs={{0,6},{2,4},{4,2},{6,0},{8,14},{10,12},{12,10},{14,8},{1,7},{3,5},... | collective-permute-start | bytes 196616 | tf_op jit(solution)/shard_map/ppermute | solution.py:141
  53.0 2.1 %collective-permute-start.12 = (bf16[128,256]{1,0:T(8,128)(2,1)S(1)}, bf16[128,256]{1,0:T(8,128)(2,1)S(1)}, u32[]{:S(2)}, u32[]{:S(2)}) collective-permute-start(bf16[128,256]{1,0:T(8,128)(2,1)S(1)} %shard_map.99.mine), channel_id=1, source_target_pairs={{0,4},{2,6},{4,0},{6,2},{8,12},{10,14},{12,8},{14,10},{1,5},{3,7},... | collective-permute-start | bytes 196616 | tf_op jit(solution)/shard_map/ppermute | solution.py:141
  56.0 1.9 %collective-permute-done.13.rest_1_ = bf16[128,256]{1,0:T(8,128)(2,1)S(1)} collective-permute-done((bf16[128,256]{1,0:T(8,128)(2,1)S(1)}, bf16[128,256]{1,0:T(8,128)(2,1)S(1)}, u32[]{:S(2)}, u32[]{:S(2)}) %collective-permute-start.13) | collective-permute-done | bytes 65568 | tf_op jit(solution)/shard_map/ppermute | solution.py:141
  57.9 1.8 %collective-permute-start.8 = (bf16[4,128,256]{2,1,0:T(8,128)(2,1)S(1)}, bf16[4,128,256]{2,1,0:T(8,128)(2,1)S(1)}, u32[]{:S(2)}, u32[]{:S(2)}) collective-permute-start(bf16[4,128,256]{2,1,0:T(8,128)(2,1)S(1)} %bitcast.33), channel_id=1, source_target_pairs={{0,12},{4,0},{8,4},{12,8},{1,13},{5,1},{9,5},{13,9},{2,14},{6,2},{... | collective-permute-start | bytes 786440 | tf_op jit(solution)/shard_map/ppermute | solution.py:32
  59.7 8.3 %collective-permute-done.12.rest_0_ = bf16[128,256]{1,0:T(8,128)(2,1)S(1)} collective-permute-done((bf16[128,256]{1,0:T(8,128)(2,1)S(1)}, bf16[128,256]{1,0:T(8,128)(2,1)S(1)}, u32[]{:S(2)}, u32[]{:S(2)}) %collective-permute-start.12) | collective-permute-done | bytes 65568 | tf_op jit(solution)/shard_map/ppermute | solution.py:141
  68.9 3.0 %collective-permute-done.9.rest_1_ = bf16[4,128,256]{2,1,0:T(8,128)(2,1)S(1)} collective-permute-done((bf16[4,128,256]{2,1,0:T(8,128)(2,1)S(1)}, bf16[4,128,256]{2,1,0:T(8,128)(2,1)S(1)}, u32[]{:S(2)}, u32[]{:S(2)}) %collective-permute-start.9) | collective-permute-done | bytes 262176 | tf_op jit(solution)/shard_map/ppermute | solution.py:32
  71.9 2.6 %shard_map.100.rest_1_ = f32[8,128,256]{2,1,0:T(8,128)S(1)} custom-call(s32[1,1]{1,0:T(1,128)S(6)} %copy.10.counts_hbm.counts, s32[1,36]{1,0:T(1,128)S(1)} %copy-done.7, s32[1,36]{1,0:T(1,128)S(1)} %copy-done.9, bf16[36,128,128]{2,1,0:T(8,128)(2,1)S(1)} %bitcast.15, bf16[8,128,256]{2,1,0:T(8,128)(2,1)S(1)} %bitcast.25, ...), custom_call_target="tpu_custom_call" | custom-call | flops 100663296 | bytes 1048576 | tf_op jit(solution)/shard_map/pallas_call | solution.py:19
  74.5 1.1 %collective-permute-done.8.rest_0_ = bf16[4,128,256]{2,1,0:T(8,128)(2,1)S(1)} collective-permute-done((bf16[4,128,256]{2,1,0:T(8,128)(2,1)S(1)}, bf16[4,128,256]{2,1,0:T(8,128)(2,1)S(1)}, u32[]{:S(2)}, u32[]{:S(2)}) %collective-permute-start.8) | collective-permute-done | bytes 262176 | tf_op jit(solution)/shard_map/ppermute | solution.py:32
  75.6 1.2 %shard_map.101.rest_1_ = f32[8,128,256]{2,1,0:T(8,128)S(1)} custom-call(s32[1,1]{1,0:T(1,128)S(6)} %copy.10.counts_hbm.counts, s32[1,36]{1,0:T(1,128)S(1)} %copy-done.7, s32[1,36]{1,0:T(1,128)S(1)} %copy-done.9, bf16[36,128,128]{2,1,0:T(8,128)(2,1)S(1)} %bitcast.16, bf16[4,128,256]{2,1,0:T(8,128)(2,1)S(1)} %collective-permute-done.8.rest_0_, ...), custom_call_target="tpu_custom_call" | custom-call | flops 100663296 | bytes 1048576 | tf_op jit(solution)/shard_map/pallas_call | solution.py:19
  76.8 2.9 %collective-permute-done.7.rest_0_ = bf16[4,128,256]{2,1,0:T(8,128)(2,1)S(1)} collective-permute-done((bf16[4,128,256]{2,1,0:T(8,128)(2,1)S(1)}, bf16[4,128,256]{2,1,0:T(8,128)(2,1)S(1)}, u32[]{:S(2)}, u32[]{:S(2)}) %collective-permute-start.7) | collective-permute-done | bytes 262176 | tf_op jit(solution)/shard_map/ppermute | solution.py:32
  79.7 2.0 %shard_map.102 = bf16[8,128,256]{2,1,0:T(8,128)(2,1)} custom-call(s32[1,1]{1,0:T(1,128)S(6)} %copy.10.counts_hbm.counts, s32[1,36]{1,0:T(1,128)S(1)} %copy-done.7, s32[1,36]{1,0:T(1,128)S(1)} %copy-done.9, bf16[36,128,128]{2,1,0:T(8,128)(2,1)S(1)} %bitcast.17, bf16[4,128,256]{2,1,0:T(8,128)(2,1)S(1)} %collective-permute-done.7.rest_0_, ...), custom_call_target="tpu_custom_call" | custom-call | flops 100663296 | bytes 1048576 | tf_op jit(solution)/shard_map/pallas_call | solution.py:19
  81.7 0.9 %shard_map.103 = bf16[1024,256]{1,0:T(8,128)(2,1)} custom-call(f32[1024,256]{1,0:T(8,128)S(1)} %get-tuple-element.29.gsum, bf16[1024,256]{1,0:T(8,128)(2,1)S(1)} %collective-permute-done.11.arrived), custom_call_target="tpu_custom_call" | custom-call | bytes 2097152 | tf_op jit(solution)/shard_map/pallas_call | solution.py:19
  (38 shorter events, 6.9 us)
Async XLA Ops:
  0.6 14.3 %collective-permute-start = (bf16[1024,256]{1,0:T(8,128)(2,1)}, bf16[1024,256]{1,0:T(8,128)(2,1)S(1)}, u32[]{:S(2)}, u32[]{:S(2)}) collective-permute-start(bf16[1024,256]{1,0:T(8,128)(2,1)} %bitcast.22), channel_id=1, source_target_pairs={{0,1},{1,0},{2,3},{3,2},{4,5},{5,4},{6,7},{7,6},{8,9},{9,8},{10,11... | collective-permute-start | bytes 1572872 | tf_op jit(solution)/shard_map/ppermute | solution.py:32
  1.8 1.3 %copy-start = (bf16[1,36,128,128]{3,2,1,0:T(8,128)(2,1)S(1)}, bf16[1,36,128,128]{3,2,1,0:T(8,128)(2,1)}, u32[]{:S(2)}) copy-start(bf16[1,36,128,128]{3,2,1,0:T(8,128)(2,1)} %param.9) | copy-start | bytes 3538948
  3.1 1.0 %copy-start.2 = (bf16[1,1024,256]{2,1,0:T(8,128)(2,1)S(1)}, bf16[1,1024,256]{2,1,0:T(8,128)(2,1)}, u32[]{:S(2)}) copy-start(bf16[1,1024,256]{2,1,0:T(8,128)(2,1)} %param.13) | copy-start | bytes 1572868
  4.1 0.7 copy-start.6
  7.9 17.7 %collective-permute-start.1 = (bf16[8,128,256]{2,1,0:T(8,128)(2,1)S(1)}, bf16[8,128,256]{2,1,0:T(8,128)(2,1)S(1)}, u32[]{:S(2)}, u32[]{:S(2)}) collective-permute-start(bf16[8,128,256]{2,1,0:T(8,128)(2,1)S(1)} %get-tuple-element.18), channel_id=1, source_target_pairs={{0,12},{4,0},{8,4},{12,8},{1,13},{5,1},{9,5},{13,9},{2,14},{6,2},{... | collective-permute-start | bytes 1572872 | tf_op jit(solution)/shard_map/ppermute | solution.py:32
  13.4 1.6 %copy-start.4 = (bf16[1,1024,256]{2,1,0:T(8,128)(2,1)S(1)}, bf16[1,1024,256]{2,1,0:T(8,128)(2,1)}, u32[]{:S(2)}) copy-start(bf16[1,1024,256]{2,1,0:T(8,128)(2,1)} %param.7) | copy-start | bytes 1572868
  13.4 1.6 %copy-start.5 = (bf16[512,256]{1,0:T(8,128)(2,1)S(1)}, bf16[512,256]{1,0:T(8,128)(2,1)}, u32[]{:S(2)}) copy-start(bf16[512,256]{1,0:T(8,128)(2,1)} %weight.3) | copy-start | bytes 786436
  13.4 23.8 %collective-permute-start.2 = (bf16[8,128,256]{2,1,0:T(8,128)(2,1)S(1)}, bf16[8,128,256]{2,1,0:T(8,128)(2,1)S(1)}, u32[]{:S(2)}, u32[]{:S(2)}) collective-permute-start(bf16[8,128,256]{2,1,0:T(8,128)(2,1)S(1)} %get-tuple-element.19), channel_id=1, source_target_pairs={{0,4},{4,8},{8,12},{12,0},{1,5},{5,9},{9,13},{13,1},{2,6},{6,10},{... | collective-permute-start | bytes 1572872 | tf_op jit(solution)/shard_map/ppermute | solution.py:32
  14.9 22.3 %copy-start.3 = (bf16[1,1024,256]{2,1,0:T(8,128)(2,1)S(1)}, bf16[1,1024,256]{2,1,0:T(8,128)(2,1)}, u32[]{:S(2)}) copy-start(bf16[1,1024,256]{2,1,0:T(8,128)(2,1)} %param.13) | copy-start | bytes 1572868
  38.0 5.0 %collective-permute-start.3 = (bf16[128,256]{1,0:T(8,128)(2,1)S(1)}, bf16[128,256]{1,0:T(8,128)(2,1)S(1)}, u32[]{:S(2)}, u32[]{:S(2)}) collective-permute-start(bf16[128,256]{1,0:T(8,128)(2,1)S(1)} %get-tuple-element.23), channel_id=1, source_target_pairs={{0,4},{2,6},{4,0},{6,2},{8,12},{10,14},{12,8},{14,10},{1,5},{3,7},... | collective-permute-start | bytes 196616 | tf_op jit(solution)/shard_map/ppermute | solution.py:141
  39.9 5.2 %collective-permute-start.4 = (bf16[128,256]{1,0:T(8,128)(2,1)S(1)}, bf16[128,256]{1,0:T(8,128)(2,1)S(1)}, u32[]{:S(2)}, u32[]{:S(2)}) collective-permute-start(bf16[128,256]{1,0:T(8,128)(2,1)S(1)} %get-tuple-element.24), channel_id=1, source_target_pairs={{0,6},{2,4},{4,2},{6,0},{8,14},{10,12},{12,10},{14,8},{1,7},{3,5},... | collective-permute-start | bytes 196616 | tf_op jit(solution)/shard_map/ppermute | solution.py:141
  41.2 4.5 %collective-permute-start.5 = (bf16[128,256]{1,0:T(8,128)(2,1)S(1)}, bf16[128,256]{1,0:T(8,128)(2,1)S(1)}, u32[]{:S(2)}, u32[]{:S(2)}) collective-permute-start(bf16[128,256]{1,0:T(8,128)(2,1)S(1)} %get-tuple-element.25), channel_id=1, source_target_pairs={{0,2},{2,0},{4,6},{6,4},{8,10},{10,8},{12,14},{14,12},{1,3},{3,1},... | collective-permute-start | bytes 196616 | tf_op jit(solution)/shard_map/ppermute | solution.py:141
  45.7 26.1 %copy-start.1 = (bf16[1,36,128,128]{3,2,1,0:T(8,128)(2,1)S(1)}, bf16[1,36,128,128]{3,2,1,0:T(8,128)(2,1)}, u32[]{:S(2)}) copy-start(bf16[1,36,128,128]{3,2,1,0:T(8,128)(2,1)} %param.9) | copy-start | bytes 3538948
  45.7 26.1 %copy-start.7 = (s32[1,36]{1,0:T(1,128)S(1)}, s32[1,36]{1,0:T(1,128)}, u32[]{:S(2)}) copy-start(s32[1,36]{1,0:T(1,128)} %target.5) | copy-start | bytes 436
  45.7 26.1 %copy-start.9 = (s32[1,36]{1,0:T(1,128)S(1)}, s32[1,36]{1,0:T(1,128)}, u32[]{:S(2)}) copy-start(s32[1,36]{1,0:T(1,128)} %source.5) | copy-start | bytes 436
  45.8 5.8 %collective-permute-start.6 = (bf16[128,256]{1,0:T(8,128)(2,1)S(1)}, bf16[128,256]{1,0:T(8,128)(2,1)S(1)}, u32[]{:S(2)}, u32[]{:S(2)}) collective-permute-start(bf16[128,256]{1,0:T(8,128)(2,1)S(1)} %shard_map.98.refs_0_), channel_id=1, source_target_pairs={{0,8},{4,12},{8,0},{12,4},{1,9},{5,13},{9,1},{13,5},{2,10},{6,14},... | collective-permute-start | bytes 196616 | tf_op jit(solution)/shard_map/ppermute | solution.py:281
  46.5 35.3 %collective-permute-start.11 = (bf16[1024,256]{1,0:T(8,128)(2,1)S(1)}, bf16[1024,256]{1,0:T(8,128)(2,1)S(1)}, u32[]{:S(2)}, u32[]{:S(2)}) collective-permute-start(bf16[1024,256]{1,0:T(8,128)(2,1)S(1)} %get-tuple-element.30), channel_id=1, source_target_pairs={{0,1},{1,0},{2,3},{3,2},{4,5},{5,4},{6,7},{7,6},{8,9},{9,8},{10,11... | collective-permute-start | bytes 1572872 | tf_op jit(solution)/shard_map/ppermute | solution.py:32
  51.6 4.3 %collective-permute-start.14 = (bf16[128,256]{1,0:T(8,128)(2,1)S(1)}, bf16[128,256]{1,0:T(8,128)(2,1)S(1)}, u32[]{:S(2)}, u32[]{:S(2)}) collective-permute-start(bf16[128,256]{1,0:T(8,128)(2,1)S(1)} %shard_map.99.mine), channel_id=1, source_target_pairs={{0,2},{2,0},{4,6},{6,4},{8,10},{10,8},{12,14},{14,12},{1,3},{3,1},... | collective-permute-start | bytes 196616 | tf_op jit(solution)/shard_map/ppermute | solution.py:141
  51.6 6.2 %collective-permute-start.13 = (bf16[128,256]{1,0:T(8,128)(2,1)S(1)}, bf16[128,256]{1,0:T(8,128)(2,1)S(1)}, u32[]{:S(2)}, u32[]{:S(2)}) collective-permute-start(bf16[128,256]{1,0:T(8,128)(2,1)S(1)} %shard_map.99.mine), channel_id=1, source_target_pairs={{0,6},{2,4},{4,2},{6,0},{8,14},{10,12},{12,10},{14,8},{1,7},{3,5},... | collective-permute-start | bytes 196616 | tf_op jit(solution)/shard_map/ppermute | solution.py:141
  53.0 15.0 %collective-permute-start.12 = (bf16[128,256]{1,0:T(8,128)(2,1)S(1)}, bf16[128,256]{1,0:T(8,128)(2,1)S(1)}, u32[]{:S(2)}, u32[]{:S(2)}) collective-permute-start(bf16[128,256]{1,0:T(8,128)(2,1)S(1)} %shard_map.99.mine), channel_id=1, source_target_pairs={{0,4},{2,6},{4,0},{6,2},{8,12},{10,14},{12,8},{14,10},{1,5},{3,7},... | collective-permute-start | bytes 196616 | tf_op jit(solution)/shard_map/ppermute | solution.py:141
  55.1 13.7 %collective-permute-start.10 = (bf16[4,128,256]{2,1,0:T(8,128)(2,1)S(1)}, bf16[4,128,256]{2,1,0:T(8,128)(2,1)S(1)}, u32[]{:S(2)}, u32[]{:S(2)}) collective-permute-start(bf16[4,128,256]{2,1,0:T(8,128)(2,1)S(1)} %bitcast.30), channel_id=1, source_target_pairs={{0,4},{4,8},{8,12},{12,0},{1,5},{5,9},{9,13},{13,1},{2,6},{6,10},{... | collective-permute-start | bytes 786440 | tf_op jit(solution)/shard_map/ppermute | solution.py:32
  55.9 16.0 %collective-permute-start.9 = (bf16[4,128,256]{2,1,0:T(8,128)(2,1)S(1)}, bf16[4,128,256]{2,1,0:T(8,128)(2,1)S(1)}, u32[]{:S(2)}, u32[]{:S(2)}) collective-permute-start(bf16[4,128,256]{2,1,0:T(8,128)(2,1)S(1)} %bitcast.32), channel_id=1, source_target_pairs={{0,4},{4,8},{8,12},{12,0},{1,5},{5,9},{9,13},{13,1},{2,6},{6,10},{... | collective-permute-start | bytes 786440 | tf_op jit(solution)/shard_map/ppermute | solution.py:32
  57.9 17.7 %collective-permute-start.8 = (bf16[4,128,256]{2,1,0:T(8,128)(2,1)S(1)}, bf16[4,128,256]{2,1,0:T(8,128)(2,1)S(1)}, u32[]{:S(2)}, u32[]{:S(2)}) collective-permute-start(bf16[4,128,256]{2,1,0:T(8,128)(2,1)S(1)} %bitcast.33), channel_id=1, source_target_pairs={{0,12},{4,0},{8,4},{12,8},{1,13},{5,1},{9,5},{13,9},{2,14},{6,2},{... | collective-permute-start | bytes 786440 | tf_op jit(solution)/shard_map/ppermute | solution.py:32
  68.0 11.7 %collective-permute-start.7 = (bf16[4,128,256]{2,1,0:T(8,128)(2,1)S(1)}, bf16[4,128,256]{2,1,0:T(8,128)(2,1)S(1)}, u32[]{:S(2)}, u32[]{:S(2)}) collective-permute-start(bf16[4,128,256]{2,1,0:T(8,128)(2,1)S(1)} %bitcast.31), channel_id=1, source_target_pairs={{0,12},{4,0},{8,4},{12,8},{1,13},{5,1},{9,5},{13,9},{2,14},{6,2},{... | collective-permute-start | bytes 786440 | tf_op jit(solution)/shard_map/ppermute | solution.py:32
  (1 other events, 0.7 us)

commit v3 on v2

--- a/solution.py
+++ b/solution.py
@@ -10,26 +10,33 @@
 F32 = jnp.float32
 BF16 = jnp.bfloat16
 UNROLL = 4
+BACK_COST, PREACT_COST, SLOPE_COST, SUM_COST, GRADS_COST = 1.0, 1.0, 0.5, 0.1, 0.5
+TRIPLET_COSTS = (2.0, 1.0, 1.0)
 VMEM = pl.BlockSpec(memory_space=pltpu.VMEM)
 SMEM = pl.BlockSpec(memory_space=pltpu.SMEM)
 HBM = pl.BlockSpec(memory_space=pltpu.HBM)
 
 
-def call(body, ins, outs, scratch=(), flops=0, nbytes=0, space=None):
+def call(body, ins, outs, scratch=(), cost=0.0, space=None, limit=32):
     return pl.pallas_call(
         body,
+        name=getattr(body, "func", body).__name__,
         in_specs=[space or (SMEM if x.dtype == jnp.int32 else VMEM) for x in ins],
         out_shape=[jax.ShapeDtypeStruct(s, d) for s, d in outs],
         out_specs=[VMEM for _ in outs],
         scratch_shapes=list(scratch),
-        cost_estimate=pl.CostEstimate(flops=flops, bytes_accessed=nbytes, transcendentals=0),
-        compiler_params=pltpu.CompilerParams(vmem_limit_bytes=32 * 1024 * 1024),
+        cost_estimate=pl.CostEstimate(flops=int(cost * 1.15e9), bytes_accessed=0, transcendentals=0),
+        compiler_params=pltpu.CompilerParams(vmem_limit_bytes=limit * 1024 * 1024),
     )(*ins)
 
 
 def shift(value, axis, steps):
     count = lax.axis_size(axis)
     return lax.ppermute(value, axis, [(i, (i + steps) % count) for i in range(count)])
+
+
+def after(value, *others):
+    return lax.optimization_barrier((value, *others))[0]
 
 
 def pick(listed, count, source, low, high):
@@ -112,7 +119,7 @@
         out[b] = acc[b].astype(out.dtype)
 
 
-def preact_body(step, mine, theirs, weight, act, factor, flipped):
+def preact_body(step, mine, theirs, weight, low_act, high_act, factor, flipped):
     rows, chans = mine.shape
     core = lax.axis_index("tensor")
     own = pl.ds(pl.multiple_of(core * chans, chans), chans)
@@ -123,10 +130,22 @@
             theirs[at], weight[other], preferred_element_type=F32
         )
         sig = 1.0 / (1.0 + jnp.exp(-pre))
-        act[at] = (pre * sig).astype(BF16)
+        act, inside = (low_act, r) if r < rows // 2 else (high_act, r - rows // 2)
+        act[pl.ds(inside, step)] = (pre * sig).astype(BF16)
         factor[at] = sig * (1.0 + pre * (1.0 - sig))
         flipped[own, at] = mine[at].T
         flipped[other, at] = theirs[at].T
+
+
+def activate_body(mine, theirs, weight, act):
+    chans = mine.shape[1]
+    core = lax.axis_index("tensor")
+    own = pl.ds(pl.multiple_of(core * chans, chans), chans)
+    other = pl.ds(pl.multiple_of((1 - core) * chans, chans), chans)
+    pre = jnp.dot(mine[...], weight[own], preferred_element_type=F32) + jnp.dot(
+        theirs[...], weight[other], preferred_element_type=F32
+    )
+    act[...] = (pre / (1.0 + jnp.exp(-pre))).astype(BF16)
 
 
 def partners():
@@ -209,10 +228,11 @@
     flat = (rows, chans)
     index = [counts, target_blocks, source_blocks, tiles]
     work = [pltpu.VMEM((nblocks + 1, tile, chans), F32), pltpu.SMEM((slots + UNROLL,), jnp.int32)]
-    unit = 2 * tile * tile * chans * slots // 3
 
     half = nblocks // 2
+    quarter = (half, tile, chans)
     theirs = shift(mine, "tensor", 1)
+    prev_rows = shift(mine[: rows // 2], "graph", 1)
 
     def back_terms(ranges, kinds):
         return call(
@@ -222,72 +242,78 @@
             work
             + [pltpu.SMEM(x.shape, jnp.int32) for x in index[:3]]
             + [pltpu.VMEM(tiles.shape, BF16), pltpu.VMEM(blocks, BF16), pltpu.SemaphoreType.DMA((5,))],
-            flops=len(ranges) * unit,
-            nbytes=4 * rows * chans,
+            cost=BACK_COST,
             space=HBM,
-        )
-
-    to_prev, to_next = back_terms((0, 2 * nblocks), (BF16, BF16))
+            limit=58,
+        )
+
+    (to_prev,) = back_terms((0,), (BF16,))
     from_next = shift(to_prev, "graph", -1)
+    to_next, back = back_terms((2 * nblocks, nblocks), (BF16, F32))
     from_prev = shift(to_next, "graph", 1)
-    (back,) = back_terms((nblocks,), (F32,))
-    act, factor, flipped = call(
+    low_act, high_act, factor, flipped = call(
         functools.partial(preact_body, 256),
         [mine, theirs, weight],
-        [(flat, BF16), (flat, F32), ((depth, rows), BF16)],
-        flops=2 * rows * depth * chans,
-        nbytes=8 * rows * chans,
-    )
-    act = act.reshape(blocks)
-    low_act, high_act = act[:half], act[half:]
-
-    def triplet(lows, pieces, start, kind):
+        [((rows // 2, chans), BF16)] * 2 + [(flat, F32), ((depth, rows), BF16)],
+        cost=PREACT_COST,
+    )
+    low_act = low_act.reshape(quarter)
+    high_act = high_act.reshape(quarter)
+    prev_high = shift(high_act, "graph", 1)
+    (prev_low,) = call(
+        activate_body,
+        [prev_rows, shift(prev_rows, "tensor", 1), weight],
+        [((rows // 2, chans), BF16)],
+        cost=PREACT_COST,
+    )
+    prev_low = prev_low.reshape(quarter)
+
+    others = partners()
+    size = depth // (len(others) + 1)
+    to_core, gsum, keep, *sends = call(
+        functools.partial(slope_body, 256),
+        [after(back, prev_low).reshape(flat), from_next.reshape(flat), from_prev.reshape(flat), factor, grads, weight, flipped],
+        [(flat, BF16), (flat, F32), ((size, chans), F32)] + [((size, chans), BF16)] * len(others),
+        [pltpu.VMEM(flat, BF16), pltpu.VMEM((depth, chans), F32)],
+        cost=SLOPE_COST,
+    )
+    arrived = [to_partner(s, *at) for s, at in zip(sends, others)]
+    next_low = shift(after(low_act, keep), "graph", -1)
+    summed = shift(to_core, "tensor", 1)
+    (grad_edges,) = call(grads_body, [gsum, summed], [(flat, BF16)], cost=GRADS_COST)
+
+    def triplet(lows, pieces, start, kind, cost):
         (acc,) = call(
             functools.partial(triplet_body, lows, nblocks),
             [*index, *pieces, start],
             [(blocks, kind)],
             work,
-            flops=unit,
-            nbytes=4 * rows * chans,
+            cost=cost,
         )
         return acc
 
-    prev_low = shift(low_act, "graph", 1)
-    others = partners()
-    size = depth // (len(others) + 1)
-    to_core, gsum, keep, *sends = call(
-        functools.partial(slope_body, 256),
-        [back.reshape(flat), from_next.reshape(flat), from_prev.reshape(flat), factor, grads, weight, flipped],
-        [(flat, BF16), (flat, F32), ((size, chans), F32)] + [((size, chans), BF16)] * len(others),
-        [pltpu.VMEM(flat, BF16), pltpu.VMEM((depth, chans), F32)],
-        flops=4 * rows * depth * chans,
-        nbytes=8 * rows * chans,
-    )
-    arrived = [to_partner(s, *at) for s, at in zip(sends, others)]
-    high_now, _ = lax.optimization_barrier((high_act, keep))
-    prev_high = shift(high_now, "graph", 1)
-    summed = shift(to_core, "tensor", 1)
-    (grad_edges,) = call(grads_body, [gsum, summed], [(flat, BF16)], nbytes=8 * rows * chans)
-
     def add_up(scale, parts):
-        return call(functools.partial(total_body, scale), parts, [((size, chans), BF16)])[0]
+        return call(functools.partial(total_body, scale), parts, [((size, chans), BF16)], cost=SUM_COST)[0]
 
     scale = float(1.0 / (ndp * edges_in.shape[0] * nz * rows) ** 0.5)
     stages = bits(nz)
-    total = add_up(1.0 if stages else scale, [keep, *arrived])
-    low_now, _ = lax.optimization_barrier((low_act, total))
-    next_low = shift(low_now, "graph", -1)
+    total = add_up(1.0 if stages else scale, [after(keep, prev_high), *arrived])
+    next_high = shift(after(high_act, total), "graph", -1)
+    acc = triplet(
+        (nblocks, nblocks + half, 0, half),
+        (low_act, high_act, prev_low, prev_high),
+        mine.reshape(blocks),
+        F32,
+        TRIPLET_COSTS[0],
+    )
     for i, bit in enumerate(stages):
         swapped = lax.ppermute(total, "graph", [(z, z ^ bit) for z in range(nz)])
-        total = add_up(scale if i + 1 == len(stages) else 1.0, [total, swapped])
-    high_now, _ = lax.optimization_barrier((high_act, total))
-    next_high = shift(high_now, "graph", -1)
+        total = add_up(scale if i + 1 == len(stages) else 1.0, [after(total, next_low, acc, grad_edges), swapped])
+    acc = triplet((2 * nblocks,), (next_low,), acc, F32, TRIPLET_COSTS[1])
     arrived = [to_partner(total, *at) for at in others]
-    (grad_weight,) = call(gather_body, [total, *arrived], [((depth, chans), F32)])
-
-    acc = triplet((nblocks, 0, half), (act, prev_low, prev_high), mine.reshape(blocks), F32)
-    acc = triplet((2 * nblocks,), (next_low,), acc, F32)
-    edges_out = triplet((2 * nblocks + half,), (next_high,), acc, BF16)
+    (grad_weight,) = call(gather_body, [after(total, next_high, acc), *arrived], [((depth, chans), F32)], cost=SUM_COST)
+
+    edges_out = triplet((2 * nblocks + half,), (next_high,), acc, BF16, TRIPLET_COSTS[2])
     return edges_out.reshape(1, rows, chans), grad_edges[None], grad_weight
 
 

time: 82.8 us -> 66.3 us (0.80)
  waiting for transfers between devices: 48.7 us -> 24.4 us
  Pallas kernels: 13.1 us -> 19.3 us
  starting transfers between devices: 15.7 us -> 20.1 us
  local copies, waits for them, and re-layouts: 3.68 us -> 1.01 us
    ppermute x6, waiting for transfers between devices: 15.1 us -> 3.91 us  [to_partner(): return lax.ppermute(value, ('graph', 'dp'), pairs)]
    ppermute x8 -> x9, waiting for transfers between devices: 28.5 us -> 20.5 us  [shift(): lax.ppermute(value, axis, [(i, (i + steps) % count) for i in range(count)])]
    pallas_call x11 -> x12, Pallas kernels: 13.1 us -> 19.3 us  [call(): pl.pallas_call(body, name=getattr(body, 'func', body).__name__, in_specs=...]
    ppermute x1, waiting for transfers between devices: 5.07 us -> 0.01 us  [shards(): swapped = lax.ppermute(total, 'graph', [(z, z ^ bit) for z in range(nz)])]
    unnamed x20 -> x14, local copies, waits for them, and re-layouts: 3.64 us -> 0.04 us
    ppermute x6, starting transfers between devices: 7.1 us -> 9.63 us  [to_partner(): return lax.ppermute(value, ('graph', 'dp'), pairs)]
    ppermute x8 -> x9, starting transfers between devices: 7.95 us -> 9.38 us  [shift(): lax.ppermute(value, axis, [(i, (i + steps) % count) for i in range(count)])]
    slice x1, local copies, waits for them, and re-layouts: 0.03 us -> 0.97 us  [shards(): prev_rows = shift(mine[:rows // 2], 'graph', 1)]
  transfers between devices with their start and end apart: 15 -> 16, of which waited for: 12 -> 7; matrix products, arithmetic and copies ran while one was open for 0% -> 0% of each run, Pallas kernels for 14% -> 28%
where the time goes in v3:
time: 66.3 us; the launch traced here: 66.2 us
  waiting for transfers between devices  24.4 us (37%)
  starting transfers between devices  20.1 us (30%)
  Pallas kernels  19.3 us (29%)
  between operations  1.46 us (2%)
  local copies, waits for them, and re-layouts  1.01 us (2%)
    ppermute x9, waiting for transfers between devices, shift(): lax.ppermute(value, axis, [(i, (i + steps) % count) for i in range(count)])  20.5 us
    pallas_call x12, Pallas kernels, call(): pl.pallas_call(body, name=getattr(body, 'func', body).__name__, in_specs=...  19.3 us
    ppermute x6, starting transfers between devices, to_partner(): return lax.ppermute(value, ('graph', 'dp'), pairs)  9.63 us
    ppermute x9, starting transfers between devices, shift(): lax.ppermute(value, axis, [(i, (i + steps) % count) for i in range(count)])  9.38 us
    ppermute x6, waiting for transfers between devices, to_partner(): return lax.ppermute(value, ('graph', 'dp'), pairs)  3.91 us
  transfers between devices with their start and end apart: 16, of which 7 were waited for; matrix products, arithmetic and copies ran while one was open for 0% of the time, Pallas kernels for 28%

profile of v3, /device:TPU:0, one launch (start us, length us, event | category | flops | bytes accessed | tf_op | source)
XLA Modules:
  0.0 66.2 jit_solution(6709136488320885156)
XLA Ops:
  0.6 1.0 %slice_bitcast_fusion = bf16[512,256]{1,0:T(8,128)(2,1)S(1)} fusion(bf16[1,1024,256]{2,1,0:T(8,128)(2,1)} %param.7), kind=kLoop, calls=%fused_computation | loop fusion | bytes 524288 | tf_op jit(solution)/shard_map/slice | solution.py:235
  1.6 3.1 %collective-permute-start.1 = (bf16[512,256]{1,0:T(8,128)(2,1)S(1)}, bf16[512,256]{1,0:T(8,128)(2,1)S(1)}, u32[]{:S(2)}, u32[]{:S(2)}) collective-permute-start(bf16[512,256]{1,0:T(8,128)(2,1)S(1)} %slice_bitcast_fusion), channel_id=1, source_target_pairs={{0,4},{4,8},{8,12},{12,0},{1,5},{5,9},{9,13},{13,1},{2,6},{6,10},{... | collective-permute-start | bytes 786440 | tf_op jit(solution)/shard_map/ppermute | solution.py:35
  5.3 3.4 %back_body.3 = bf16[8,128,256]{2,1,0:T(8,128)(2,1)} custom-call(s32[1,1]{1,0:T(1,128)S(6)} %copy.10.counts_hbm.counts, s32[1,36]{1,0:T(1,128)} %target.5, s32[1,36]{1,0:T(1,128)} %source.5, bf16[36,128,128]{2,1,0:T(8,128)(2,1)} %bitcast.24, bf16[8,128,256]{2,1,0:T(8,128)(2,1)} %bitcast.16), custom_call_target="tpu_custom_call" | custom-call | flops 1150000000 | tf_op jit(solution)/shard_map/back_body/pallas_call | solution.py:21
  8.8 1.9 %collective-permute-start.3 = (bf16[8,128,256]{2,1,0:T(8,128)(2,1)}, bf16[8,128,256]{2,1,0:T(8,128)(2,1)S(1)}, u32[]{:S(2)}, u32[]{:S(2)}) collective-permute-start(bf16[8,128,256]{2,1,0:T(8,128)(2,1)} %back_body.3), channel_id=1, source_target_pairs={{0,12},{4,0},{8,4},{12,8},{1,13},{5,1},{9,5},{13,9},{2,14},{6,2},{... | collective-permute-start | bytes 1572872 | tf_op jit(solution)/shard_map/ppermute | solution.py:35
  10.7 4.9 %back_body.2 = (bf16[8,128,256]{2,1,0:T(8,128)(2,1)}, f32[8,128,256]{2,1,0:T(8,128)}) custom-call(s32[1,1]{1,0:T(1,128)S(6)} %copy.10.counts_hbm.counts, s32[1,36]{1,0:T(1,128)} %target.5, s32[1,36]{1,0:T(1,128)} %source.5, bf16[36,128,128]{2,1,0:T(8,128)(2,1)} %bitcast.25, bf16[8,128,256]{2,1,0:T(8,128)(2,1)} %bitcast.17), custom_call_target="tpu_custom_call" | custom-call | flops 1150000000 | tf_op jit(solution)/shard_map/back_body/pallas_call | solution.py:21
  16.0 0.7 %preact_body.1 = (bf16[512,256]{1,0:T(8,128)(2,1)S(1)}, bf16[512,256]{1,0:T(8,128)(2,1)S(1)}, f32[1024,256]{1,0:T(8,128)S(1)}, bf16[512,1024]{1,0:T(8,128)(2,1)S(1)}) custom-call(bf16[1024,256]{1,0:T(8,128)(2,1)S(1)} %bitcast.22, bf16[1024,256]{1,0:T(8,128)(2,1)S(1)} %collective-permute-done.theirs, bf16[512,256]{1,0:T(8,128)(2,1)S(1)} %copy-done.2), custom_call_target="tpu_custom_call" | custom-call | flops 1150000000 | tf_op jit(solution)/shard_map/preact_body/pallas_call | solution.py:21
  17.6 6.6 %collective-permute-done.3 = bf16[8,128,256]{2,1,0:T(8,128)(2,1)S(1)} collective-permute-done((bf16[8,128,256]{2,1,0:T(8,128)(2,1)}, bf16[8,128,256]{2,1,0:T(8,128)(2,1)S(1)}, u32[]{:S(2)}, u32[]{:S(2)}) %collective-permute-start.3) | collective-permute-done | bytes 524320 | tf_op jit(solution)/shard_map/ppermute | solution.py:35
  24.2 12.2 %collective-permute-done.4 = bf16[8,128,256]{2,1,0:T(8,128)(2,1)S(1)} collective-permute-done((bf16[8,128,256]{2,1,0:T(8,128)(2,1)}, bf16[8,128,256]{2,1,0:T(8,128)(2,1)S(1)}, u32[]{:S(2)}, u32[]{:S(2)}) %collective-permute-start.4) | collective-permute-done | bytes 524320 | tf_op jit(solution)/shard_map/ppermute | solution.py:35
  36.5 0.9 %slope_body.1 = (bf16[1024,256]{1,0:T(8,128)(2,1)S(1)}, f32[1024,256]{1,0:T(8,128)S(1)}, f32[128,256]{1,0:T(8,128)S(1)}, bf16[128,256]{1,0:T(8,128)(2,1)S(1)}, b...) custom-call(f32[1024,256]{1,0:T(8,128)S(1)} %bitcast.15, bf16[1024,256]{1,0:T(8,128)(2,1)S(1)} %bitcast.19, ...), custom_call_target="tpu_custom_call" | custom-call | flops 575000000 | tf_op jit(solution)/shard_map/slope_body/pallas_call | solution.py:21
  37.9 2.6 %collective-permute-start.7 = (bf16[128,256]{1,0:T(8,128)(2,1)S(1)}, bf16[128,256]{1,0:T(8,128)(2,1)S(1)}, u32[]{:S(2)}, u32[]{:S(2)}) collective-permute-start(bf16[128,256]{1,0:T(8,128)(2,1)S(1)} %get-tuple-element.30), channel_id=1, source_target_pairs={{0,6},{2,4},{4,2},{6,0},{8,14},{10,12},{12,10},{14,8},{1,7},{3,5},... | collective-permute-start | bytes 196616 | tf_op jit(solution)/shard_map/ppermute | solution.py:160
  40.5 0.5 collective-permute-start.8
  41.0 1.1 %collective-permute-done.5.rest_3_ = bf16[4,128,256]{2,1,0:T(8,128)(2,1)S(1)} collective-permute-done((bf16[4,128,256]{2,1,0:T(8,128)(2,1)S(1)}, bf16[4,128,256]{2,1,0:T(8,128)(2,1)S(1)}, u32[]{:S(2)}, u32[]{:S(2)}) %collective-permute-start.5) | collective-permute-done | bytes 262176 | tf_op jit(solution)/shard_map/ppermute | solution.py:35
  42.1 1.9 %collective-permute-start.10 = (bf16[4,128,256]{2,1,0:T(8,128)(2,1)S(1)}, bf16[4,128,256]{2,1,0:T(8,128)(2,1)S(1)}, u32[]{:S(2)}, u32[]{:S(2)}) collective-permute-start(bf16[4,128,256]{2,1,0:T(8,128)(2,1)S(1)} %bitcast.32), channel_id=1, source_target_pairs={{0,12},{4,0},{8,4},{12,8},{1,13},{5,1},{9,5},{13,9},{2,14},{6,2},{... | collective-permute-start | bytes 786440 | tf_op jit(solution)/shard_map/ppermute | solution.py:35
  44.0 1.6 %collective-permute-done.7.refs_2_ = bf16[128,256]{1,0:T(8,128)(2,1)S(1)} collective-permute-done((bf16[128,256]{1,0:T(8,128)(2,1)S(1)}, bf16[128,256]{1,0:T(8,128)(2,1)S(1)}, u32[]{:S(2)}, u32[]{:S(2)}) %collective-permute-start.7) | collective-permute-done | bytes 65568 | tf_op jit(solution)/shard_map/ppermute | solution.py:160
  45.5 0.6 collective-permute-done.8.refs_3_
  46.2 1.0 %collective-permute-start.12 = (bf16[128,256]{1,0:T(8,128)(2,1)S(1)}, bf16[128,256]{1,0:T(8,128)(2,1)S(1)}, u32[]{:S(2)}, u32[]{:S(2)}) collective-permute-start(bf16[128,256]{1,0:T(8,128)(2,1)S(1)} %total_body.2.refs_0_), channel_id=1, source_target_pairs={{0,8},{4,12},{8,0},{12,4},{1,9},{5,13},{9,1},{13,5},{2,10},{6,14},... | collective-permute-start | bytes 196616 | tf_op jit(solution)/shard_map/ppermute | solution.py:310
  47.2 2.0 %collective-permute-start.9 = (bf16[4,128,256]{2,1,0:T(8,128)(2,1)S(1)}, bf16[4,128,256]{2,1,0:T(8,128)(2,1)S(1)}, u32[]{:S(2)}, u32[]{:S(2)}) collective-permute-start(bf16[4,128,256]{2,1,0:T(8,128)(2,1)S(1)} %bitcast.30), channel_id=1, source_target_pairs={{0,12},{4,0},{8,4},{12,8},{1,13},{5,1},{9,5},{13,9},{2,14},{6,2},{... | collective-permute-start | bytes 786440 | tf_op jit(solution)/shard_map/ppermute | solution.py:35
  49.3 3.6 %triplet_body.3.rest_1_ = f32[8,128,256]{2,1,0:T(8,128)S(1)} custom-call(s32[1,1]{1,0:T(1,128)S(6)} %copy.10.counts_hbm.counts, s32[1,36]{1,0:T(1,128)S(1)} %copy-done.5, s32[1,36]{1,0:T(1,128)S(1)} %copy-done.6, bf16[36,128,128]{2,1,0:T(8,128)(2,1)S(1)} %bitcast.26, bf16[4,128,256]{2,1,0:T(8,128)(2,1)S(1)} %bitcast.33, bf16[4,128,256]{2,1,0:T(8,128)(2,1)S(1)} %bitcast.31, ...), custom_call_target="tpu_custom_call" | custom-call | flops 2300000000 | tf_op jit(solution)/shard_map/triplet_body/pallas_call | solution.py:21
  52.9 1.7 %triplet_body.4.rest_1_ = f32[8,128,256]{2,1,0:T(8,128)S(1)} custom-call(s32[1,1]{1,0:T(1,128)S(6)} %copy.10.counts_hbm.counts, s32[1,36]{1,0:T(1,128)S(1)} %copy-done.5, s32[1,36]{1,0:T(1,128)S(1)} %copy-done.6, bf16[36,128,128]{2,1,0:T(8,128)(2,1)S(1)} %bitcast.27, bf16[4,128,256]{2,1,0:T(8,128)(2,1)S(1)} %collective-permute-done.10.rest_0_, ...), custom_call_target="tpu_custom_call" | custom-call | flops 1150000000 | tf_op jit(solution)/shard_map/triplet_body/pallas_call | solution.py:21
  54.6 0.9 %grads_body.1 = bf16[1024,256]{1,0:T(8,128)(2,1)} custom-call(f32[1024,256]{1,0:T(8,128)S(1)} %get-tuple-element.35.gsum, bf16[1024,256]{1,0:T(8,128)(2,1)S(1)} %collective-permute-done.11.arrived), custom_call_target="tpu_custom_call" | custom-call | flops 575000000 | tf_op jit(solution)/shard_map/grads_body/pallas_call | solution.py:21
  56.0 5.1 %collective-permute-start.14 = (bf16[128,256]{1,0:T(8,128)(2,1)S(1)}, bf16[128,256]{1,0:T(8,128)(2,1)S(1)}, u32[]{:S(2)}, u32[]{:S(2)}) collective-permute-start(bf16[128,256]{1,0:T(8,128)(2,1)S(1)} %total_body.3.mine), channel_id=1, source_target_pairs={{0,6},{2,4},{4,2},{6,0},{8,14},{10,12},{12,10},{14,8},{1,7},{3,5},... | collective-permute-start | bytes 196616 | tf_op jit(solution)/shard_map/ppermute | solution.py:160
  61.6 2.0 %triplet_body.5 = bf16[8,128,256]{2,1,0:T(8,128)(2,1)} custom-call(s32[1,1]{1,0:T(1,128)S(6)} %copy.10.counts_hbm.counts, s32[1,36]{1,0:T(1,128)S(1)} %copy-done.5, s32[1,36]{1,0:T(1,128)S(1)} %copy-done.6, bf16[36,128,128]{2,1,0:T(8,128)(2,1)S(1)} %bitcast.28, bf16[4,128,256]{2,1,0:T(8,128)(2,1)S(1)} %collective-permute-done.9.rest_0_, ...), custom_call_target="tpu_custom_call" | custom-call | flops 1150000000 | tf_op jit(solution)/shard_map/triplet_body/pallas_call | solution.py:21
  63.6 1.8 %collective-permute-done.13.rest_0_ = bf16[128,256]{1,0:T(8,128)(2,1)S(1)} collective-permute-done((bf16[128,256]{1,0:T(8,128)(2,1)S(1)}, bf16[128,256]{1,0:T(8,128)(2,1)S(1)}, u32[]{:S(2)}, u32[]{:S(2)}) %collective-permute-start.13) | collective-permute-done | bytes 65568 | tf_op jit(solution)/shard_map/ppermute | solution.py:160
  65.4 0.8 %gather_body.1 = f32[512,256]{1,0:T(8,128)} custom-call(bf16[128,256]{1,0:T(8,128)(2,1)S(1)} %total_body.3.mine, bf16[128,256]{1,0:T(8,128)(2,1)S(1)} %collective-permute-done.13.rest_0_, bf16[128,256]{1,0:T(8,128)(2,1)S(1)} %collective-permute-done.14.rest_1_, bf16[128,256]{1,0:T(8,128)(2,1)S(1)} %collective-permute-done.15.rest_2_), custom_call_target="tpu_custom_call" | custom-call | flops 115000000 | tf_op jit(solution)/shard_map/gather_body/pallas_call | solution.py:21
  (35 shorter events, 2.8 us)
Async XLA Ops:
  1.6 14.1 %collective-permute-start.1 = (bf16[512,256]{1,0:T(8,128)(2,1)S(1)}, bf16[512,256]{1,0:T(8,128)(2,1)S(1)}, u32[]{:S(2)}, u32[]{:S(2)}) collective-permute-start(bf16[512,256]{1,0:T(8,128)(2,1)S(1)} %slice_bitcast_fusion), channel_id=1, source_target_pairs={{0,4},{4,8},{8,12},{12,0},{1,5},{5,9},{9,13},{13,1},{2,6},{6,10},{... | collective-permute-start | bytes 786440 | tf_op jit(solution)/shard_map/ppermute | solution.py:35
  4.7 11.3 %collective-permute-start = (bf16[1024,256]{1,0:T(8,128)(2,1)}, bf16[1024,256]{1,0:T(8,128)(2,1)S(1)}, u32[]{:S(2)}, u32[]{:S(2)}) collective-permute-start(bf16[1024,256]{1,0:T(8,128)(2,1)} %bitcast.21), channel_id=1, source_target_pairs={{0,1},{1,0},{2,3},{3,2},{4,5},{5,4},{6,7},{7,6},{8,9},{9,8},{10,11... | collective-permute-start | bytes 1572872 | tf_op jit(solution)/shard_map/ppermute | solution.py:35
  8.7 7.2 %copy-start.2 = (bf16[512,256]{1,0:T(8,128)(2,1)S(1)}, bf16[512,256]{1,0:T(8,128)(2,1)}, u32[]{:S(2)}) copy-start(bf16[512,256]{1,0:T(8,128)(2,1)} %weight.5) | copy-start | bytes 786436
  8.7 7.2 %copy-start.3 = (bf16[1,1024,256]{2,1,0:T(8,128)(2,1)S(1)}, bf16[1,1024,256]{2,1,0:T(8,128)(2,1)}, u32[]{:S(2)}) copy-start(bf16[1,1024,256]{2,1,0:T(8,128)(2,1)} %param.7) | copy-start | bytes 1572868
  8.8 15.5 %collective-permute-start.3 = (bf16[8,128,256]{2,1,0:T(8,128)(2,1)}, bf16[8,128,256]{2,1,0:T(8,128)(2,1)S(1)}, u32[]{:S(2)}, u32[]{:S(2)}) collective-permute-start(bf16[8,128,256]{2,1,0:T(8,128)(2,1)} %back_body.3), channel_id=1, source_target_pairs={{0,12},{4,0},{8,4},{12,8},{1,13},{5,1},{9,5},{13,9},{2,14},{6,2},{... | collective-permute-start | bytes 1572872 | tf_op jit(solution)/shard_map/ppermute | solution.py:35
  15.6 20.9 %collective-permute-start.4 = (bf16[8,128,256]{2,1,0:T(8,128)(2,1)}, bf16[8,128,256]{2,1,0:T(8,128)(2,1)S(1)}, u32[]{:S(2)}, u32[]{:S(2)}) collective-permute-start(bf16[8,128,256]{2,1,0:T(8,128)(2,1)} %get-tuple-element.24), channel_id=1, source_target_pairs={{0,4},{4,8},{8,12},{12,0},{1,5},{5,9},{9,13},{13,1},{2,6},{6,10},{... | collective-permute-start | bytes 1572872 | tf_op jit(solution)/shard_map/ppermute | solution.py:35
  15.7 1.6 %collective-permute-start.2 = (bf16[512,256]{1,0:T(8,128)(2,1)S(1)}, bf16[512,256]{1,0:T(8,128)(2,1)S(1)}, u32[]{:S(2)}, u32[]{:S(2)}) collective-permute-start(bf16[512,256]{1,0:T(8,128)(2,1)S(1)} %collective-permute-done.1.mine), channel_id=1, source_target_pairs={{0,1},{1,0},{2,3},{3,2},{4,5},{5,4},{6,7},{7,6},{8,9},{9,8},{10,11... | collective-permute-start | bytes 786440 | tf_op jit(solution)/shard_map/ppermute | solution.py:35
  16.7 19.8 %copy-start = (f32[8,128,256]{2,1,0:T(8,128)S(1)}, f32[8,128,256]{2,1,0:T(8,128)}, u32[]{:S(2)}) copy-start(f32[8,128,256]{2,1,0:T(8,128)} %get-tuple-element.23) | copy-start | bytes 3145732
  16.7 19.8 %copy-start.1 = (bf16[1,1024,256]{2,1,0:T(8,128)(2,1)S(1)}, bf16[1,1024,256]{2,1,0:T(8,128)(2,1)}, u32[]{:S(2)}) copy-start(bf16[1,1024,256]{2,1,0:T(8,128)(2,1)} %param.13) | copy-start | bytes 1572868
  16.7 25.4 %collective-permute-start.5 = (bf16[4,128,256]{2,1,0:T(8,128)(2,1)S(1)}, bf16[4,128,256]{2,1,0:T(8,128)(2,1)S(1)}, u32[]{:S(2)}, u32[]{:S(2)}) collective-permute-start(bf16[4,128,256]{2,1,0:T(8,128)(2,1)S(1)} %bitcast.29), channel_id=1, source_target_pairs={{0,4},{4,8},{8,12},{12,0},{1,5},{5,9},{9,13},{13,1},{2,6},{6,10},{... | collective-permute-start | bytes 786440 | tf_op jit(solution)/shard_map/ppermute | solution.py:35
  36.5 12.8 %copy-start.4 = (bf16[1,36,128,128]{3,2,1,0:T(8,128)(2,1)S(1)}, bf16[1,36,128,128]{3,2,1,0:T(8,128)(2,1)}, u32[]{:S(2)}) copy-start(bf16[1,36,128,128]{3,2,1,0:T(8,128)(2,1)} %param.9) | copy-start | bytes 3538948
  36.5 12.8 %copy-start.5 = (s32[1,36]{1,0:T(1,128)S(1)}, s32[1,36]{1,0:T(1,128)}, u32[]{:S(2)}) copy-start(s32[1,36]{1,0:T(1,128)} %target.5) | copy-start | bytes 436
  36.5 12.8 %copy-start.6 = (s32[1,36]{1,0:T(1,128)S(1)}, s32[1,36]{1,0:T(1,128)}, u32[]{:S(2)}) copy-start(s32[1,36]{1,0:T(1,128)} %source.5) | copy-start | bytes 436
  37.4 17.2 %collective-permute-start.11 = (bf16[1024,256]{1,0:T(8,128)(2,1)S(1)}, bf16[1024,256]{1,0:T(8,128)(2,1)S(1)}, u32[]{:S(2)}, u32[]{:S(2)}) collective-permute-start(bf16[1024,256]{1,0:T(8,128)(2,1)S(1)} %get-tuple-element.36), channel_id=1, source_target_pairs={{0,1},{1,0},{2,3},{3,2},{4,5},{5,4},{6,7},{7,6},{8,9},{9,8},{10,11... | collective-permute-start | bytes 1572872 | tf_op jit(solution)/shard_map/ppermute | solution.py:35
  37.5 6.5 %collective-permute-start.6 = (bf16[128,256]{1,0:T(8,128)(2,1)S(1)}, bf16[128,256]{1,0:T(8,128)(2,1)S(1)}, u32[]{:S(2)}, u32[]{:S(2)}) collective-permute-start(bf16[128,256]{1,0:T(8,128)(2,1)S(1)} %get-tuple-element.29), channel_id=1, source_target_pairs={{0,4},{2,6},{4,0},{6,2},{8,12},{10,14},{12,8},{14,10},{1,5},{3,7},... | collective-permute-start | bytes 196616 | tf_op jit(solution)/shard_map/ppermute | solution.py:160
  37.9 7.6 %collective-permute-start.7 = (bf16[128,256]{1,0:T(8,128)(2,1)S(1)}, bf16[128,256]{1,0:T(8,128)(2,1)S(1)}, u32[]{:S(2)}, u32[]{:S(2)}) collective-permute-start(bf16[128,256]{1,0:T(8,128)(2,1)S(1)} %get-tuple-element.30), channel_id=1, source_target_pairs={{0,6},{2,4},{4,2},{6,0},{8,14},{10,12},{12,10},{14,8},{1,7},{3,5},... | collective-permute-start | bytes 196616 | tf_op jit(solution)/shard_map/ppermute | solution.py:160
  40.5 5.6 %collective-permute-start.8 = (bf16[128,256]{1,0:T(8,128)(2,1)S(1)}, bf16[128,256]{1,0:T(8,128)(2,1)S(1)}, u32[]{:S(2)}, u32[]{:S(2)}) collective-permute-start(bf16[128,256]{1,0:T(8,128)(2,1)S(1)} %get-tuple-element.31), channel_id=1, source_target_pairs={{0,2},{2,0},{4,6},{6,4},{8,10},{10,8},{12,14},{14,12},{1,3},{3,1},... | collective-permute-start | bytes 196616 | tf_op jit(solution)/shard_map/ppermute | solution.py:160
  42.1 10.8 %collective-permute-start.10 = (bf16[4,128,256]{2,1,0:T(8,128)(2,1)S(1)}, bf16[4,128,256]{2,1,0:T(8,128)(2,1)S(1)}, u32[]{:S(2)}, u32[]{:S(2)}) collective-permute-start(bf16[4,128,256]{2,1,0:T(8,128)(2,1)S(1)} %bitcast.32), channel_id=1, source_target_pairs={{0,12},{4,0},{8,4},{12,8},{1,13},{5,1},{9,5},{13,9},{2,14},{6,2},{... | collective-permute-start | bytes 786440 | tf_op jit(solution)/shard_map/ppermute | solution.py:35
  46.2 9.3 %collective-permute-start.12 = (bf16[128,256]{1,0:T(8,128)(2,1)S(1)}, bf16[128,256]{1,0:T(8,128)(2,1)S(1)}, u32[]{:S(2)}, u32[]{:S(2)}) collective-permute-start(bf16[128,256]{1,0:T(8,128)(2,1)S(1)} %total_body.2.refs_0_), channel_id=1, source_target_pairs={{0,8},{4,12},{8,0},{12,4},{1,9},{5,13},{9,1},{13,5},{2,10},{6,14},... | collective-permute-start | bytes 196616 | tf_op jit(solution)/shard_map/ppermute | solution.py:310
  47.2 14.4 %collective-permute-start.9 = (bf16[4,128,256]{2,1,0:T(8,128)(2,1)S(1)}, bf16[4,128,256]{2,1,0:T(8,128)(2,1)S(1)}, u32[]{:S(2)}, u32[]{:S(2)}) collective-permute-start(bf16[4,128,256]{2,1,0:T(8,128)(2,1)S(1)} %bitcast.30), channel_id=1, source_target_pairs={{0,12},{4,0},{8,4},{12,8},{1,13},{5,1},{9,5},{13,9},{2,14},{6,2},{... | collective-permute-start | bytes 786440 | tf_op jit(solution)/shard_map/ppermute | solution.py:35
  55.5 8.1 %collective-permute-start.15 = (bf16[128,256]{1,0:T(8,128)(2,1)S(1)}, bf16[128,256]{1,0:T(8,128)(2,1)S(1)}, u32[]{:S(2)}, u32[]{:S(2)}) collective-permute-start(bf16[128,256]{1,0:T(8,128)(2,1)S(1)} %total_body.3.mine), channel_id=1, source_target_pairs={{0,2},{2,0},{4,6},{6,4},{8,10},{10,8},{12,14},{14,12},{1,3},{3,1},... | collective-permute-start | bytes 196616 | tf_op jit(solution)/shard_map/ppermute | solution.py:160
  56.0 7.6 %collective-permute-start.14 = (bf16[128,256]{1,0:T(8,128)(2,1)S(1)}, bf16[128,256]{1,0:T(8,128)(2,1)S(1)}, u32[]{:S(2)}, u32[]{:S(2)}) collective-permute-start(bf16[128,256]{1,0:T(8,128)(2,1)S(1)} %total_body.3.mine), channel_id=1, source_target_pairs={{0,6},{2,4},{4,2},{6,0},{8,14},{10,12},{12,10},{14,8},{1,7},{3,5},... | collective-permute-start | bytes 196616 | tf_op jit(solution)/shard_map/ppermute | solution.py:160
  61.1 4.3 %collective-permute-start.13 = (bf16[128,256]{1,0:T(8,128)(2,1)S(1)}, bf16[128,256]{1,0:T(8,128)(2,1)S(1)}, u32[]{:S(2)}, u32[]{:S(2)}) collective-permute-start(bf16[128,256]{1,0:T(8,128)(2,1)S(1)} %total_body.3.mine), channel_id=1, source_target_pairs={{0,4},{2,6},{4,0},{6,2},{8,12},{10,14},{12,8},{14,10},{1,5},{3,7},... | collective-permute-start | bytes 196616 | tf_op jit(solution)/shard_map/ppermute | solution.py:160

commit v4 on v2

--- a/solution.py
+++ b/solution.py
@@ -10,21 +10,36 @@
 F32 = jnp.float32
 BF16 = jnp.bfloat16
 UNROLL = 4
+LEAD = 5
+FIRST = 4
+BACK_COST, PREACT_COST, SLOPE_COST, SUM_COST, GATHER_COST, GRADS_COST = 1.0, 1.0, 0.5, 2.0, 3.0, 0.5
+TICK_COSTS = (3.0, 0.3)
+TRIPLET_COSTS = (0.5, 0.3, 0.3, 6.0)
 VMEM = pl.BlockSpec(memory_space=pltpu.VMEM)
 SMEM = pl.BlockSpec(memory_space=pltpu.SMEM)
 HBM = pl.BlockSpec(memory_space=pltpu.HBM)
-
-
-def call(body, ins, outs, scratch=(), flops=0, nbytes=0, space=None):
+ANY = pl.BlockSpec(memory_space=pl.ANY)
+
+
+def call(body, ins, outs, scratch=(), cost=0.0, space=None, limit=32, waits=(), carried=()):
+    n, extra = len(ins), len(waits) + len(carried)
+
+    def kernel(*refs):
+        results = refs[n + extra :]
+        body(*refs[:n], *results[: len(outs)], *results[len(outs) + len(carried) :])
+
     return pl.pallas_call(
-        body,
-        in_specs=[space or (SMEM if x.dtype == jnp.int32 else VMEM) for x in ins],
-        out_shape=[jax.ShapeDtypeStruct(s, d) for s, d in outs],
-        out_specs=[VMEM for _ in outs],
+        kernel,
+        name=getattr(body, "func", body).__name__,
+        in_specs=[space or (SMEM if x.dtype == jnp.int32 else VMEM) for x in ins] + [ANY] * extra,
+        out_shape=[jax.ShapeDtypeStruct(s, d) for s, d in outs]
+        + [jax.ShapeDtypeStruct(x.shape, x.dtype) for x in carried],
+        out_specs=[VMEM for _ in outs] + [ANY for _ in carried],
         scratch_shapes=list(scratch),
-        cost_estimate=pl.CostEstimate(flops=flops, bytes_accessed=nbytes, transcendentals=0),
-        compiler_params=pltpu.CompilerParams(vmem_limit_bytes=32 * 1024 * 1024),
-    )(*ins)
+        input_output_aliases={n + len(waits) + i: len(outs) + i for i in range(len(carried))},
+        cost_estimate=pl.CostEstimate(flops=int(cost * 1.15e9), bytes_accessed=0, transcendentals=0),
+        compiler_params=pltpu.CompilerParams(vmem_limit_bytes=limit * 1024 * 1024),
+    )(*ins, *waits, *carried)
 
 
 def shift(value, axis, steps):
@@ -35,13 +50,12 @@
 def pick(listed, count, source, low, high):
     slots = source.shape[1]
 
-    def step(k, found):
+    found = jnp.int32(0)
+    for k in range(slots):
         listed[found] = k
         s = source[0, k]
         inside = (k < count) & (s >= low) & (s < high)
-        return found + inside.astype(jnp.int32)
-
-    found = lax.fori_loop(0, slots, step, jnp.int32(0))
+        found = found + inside.astype(jnp.int32)
     for j in range(UNROLL):
         listed[found + j] = 0
     return found
@@ -76,12 +90,15 @@
     for copy in copies:
         copy.start()
     acc[...] = jnp.zeros_like(acc)
-    for copy in copies:
+    for copy in copies[:3]:
         copy.wait()
     for low, out in zip(ranges, outs):
         if low != ranges[0]:
             acc[...] = jnp.zeros_like(acc)
         found = pick(listed, counts[0, 0], source, low, low + nblocks)
+        if low == ranges[0]:
+            for copy in copies[3:]:
+                copy.wait()
 
         def step(k, valid):
             at = jnp.where(valid, source[0, k] - low, nblocks)
@@ -112,7 +129,7 @@
         out[b] = acc[b].astype(out.dtype)
 
 
-def preact_body(step, mine, theirs, weight, act, factor, flipped):
+def preact_body(step, mine, theirs, weight, act, factor, flipped, up, *down):
     rows, chans = mine.shape
     core = lax.axis_index("tensor")
     own = pl.ds(pl.multiple_of(core * chans, chans), chans)
@@ -127,6 +144,26 @@
         factor[at] = sig * (1.0 + pre * (1.0 - sig))
         flipped[own, at] = mine[at].T
         flipped[other, at] = theirs[at].T
+    up[...] = act[pl.ds(rows - up.shape[0], up.shape[0])]
+    begin = 0
+    for piece in down:
+        piece[...] = act[pl.ds(begin, piece.shape[0])]
+        begin += piece.shape[0]
+
+
+def tick_body(out):
+    out[...] = jnp.zeros_like(out)
+
+
+def activate_body(mine, theirs, weight, act):
+    chans = mine.shape[1]
+    core = lax.axis_index("tensor")
+    own = pl.ds(pl.multiple_of(core * chans, chans), chans)
+    other = pl.ds(pl.multiple_of((1 - core) * chans, chans), chans)
+    pre = jnp.dot(mine[...], weight[own], preferred_element_type=F32) + jnp.dot(
+        theirs[...], weight[other], preferred_element_type=F32
+    )
+    act[...] = (pre / (1.0 + jnp.exp(-pre))).astype(BF16)
 
 
 def partners():
@@ -139,6 +176,10 @@
         (z * ndp + d, (z ^ flip) * ndp + (d + steps) % ndp) for z in range(nz) for d in range(ndp)
     ]
     return lax.ppermute(value, ("graph", "dp"), pairs)
+
+
+def swap(value, bit):
+    return lax.ppermute(value, "graph", [(z, z ^ bit) for z in range(lax.axis_size("graph"))])
 
 
 def place(flip, steps, size):
@@ -174,7 +215,8 @@
         send[...] = part[place(flip, steps, size)].astype(BF16)
 
 
-def grads_body(gsum, arrived, out):
+def grads_body(gsum, arrived, out, token):
+    token[...] = jnp.zeros_like(token)
     out[...] = (gsum[...] + arrived[...].astype(F32)).astype(BF16)
 
 
@@ -209,12 +251,12 @@
     flat = (rows, chans)
     index = [counts, target_blocks, source_blocks, tiles]
     work = [pltpu.VMEM((nblocks + 1, tile, chans), F32), pltpu.SMEM((slots + UNROLL,), jnp.int32)]
-    unit = 2 * tile * tile * chans * slots // 3
-
-    half = nblocks // 2
+
     theirs = shift(mine, "tensor", 1)
-
-    def back_terms(ranges, kinds):
+    lead = min(LEAD, nblocks - 1)
+    prev_rows = shift(mine[: lead * tile], "graph", 1)
+
+    def back_terms(ranges, kinds, waits=()):
         return call(
             functools.partial(back_body, ranges, nblocks),
             [*index, grads.reshape(blocks)],
@@ -222,72 +264,92 @@
             work
             + [pltpu.SMEM(x.shape, jnp.int32) for x in index[:3]]
             + [pltpu.VMEM(tiles.shape, BF16), pltpu.VMEM(blocks, BF16), pltpu.SemaphoreType.DMA((5,))],
-            flops=len(ranges) * unit,
-            nbytes=4 * rows * chans,
+            cost=BACK_COST,
             space=HBM,
-        )
-
-    to_prev, to_next = back_terms((0, 2 * nblocks), (BF16, BF16))
-    from_next = shift(to_prev, "graph", -1)
-    from_prev = shift(to_next, "graph", 1)
-    (back,) = back_terms((nblocks,), (F32,))
-    act, factor, flipped = call(
-        functools.partial(preact_body, 256),
-        [mine, theirs, weight],
-        [(flat, BF16), (flat, F32), ((depth, rows), BF16)],
-        flops=2 * rows * depth * chans,
-        nbytes=8 * rows * chans,
-    )
-    act = act.reshape(blocks)
-    low_act, high_act = act[:half], act[half:]
-
-    def triplet(lows, pieces, start, kind):
-        (acc,) = call(
+            limit=58,
+            waits=waits,
+        )
+
+    def tick(cost, *waits):
+        return call(tick_body, [], [((8, 128), F32)], cost=cost, waits=waits)[0]
+
+    def triplet(lows, pieces, start, kind, cost):
+        return call(
             functools.partial(triplet_body, lows, nblocks),
             [*index, *pieces, start],
             [(blocks, kind)],
             work,
-            flops=unit,
-            nbytes=4 * rows * chans,
-        )
-        return acc
-
-    prev_low = shift(low_act, "graph", 1)
+            cost=cost,
+        )[0]
+
+    (to_prev,) = back_terms((0,), (BF16,))
+    from_next = shift(to_prev, "graph", -1)
+    to_next, back = back_terms((2 * nblocks, nblocks), (BF16, F32), [to_prev])
+    from_prev = shift(to_next, "graph", 1)
+    cuts = [0, min(FIRST, nblocks - 1), nblocks]
+    sizes = [nblocks - lead] + [high - low for low, high in zip(cuts, cuts[1:])]
+    act, factor, flipped, *sent = call(
+        functools.partial(preact_body, 256),
+        [mine, theirs, weight],
+        [(flat, BF16), (flat, F32), ((depth, rows), BF16)] + [((n * tile, chans), BF16) for n in sizes],
+        cost=PREACT_COST,
+    )
+    up, first, second = [x.reshape(-1, tile, chans) for x in sent]
+    prev_high = shift(up, "graph", 1)
+    (prev_low,) = call(
+        activate_body,
+        [prev_rows, shift(prev_rows, "tensor", 1), weight],
+        [((lead * tile, chans), BF16)],
+        cost=PREACT_COST,
+    )
+    prev_low = prev_low.reshape(lead, tile, chans)
     others = partners()
     size = depth // (len(others) + 1)
-    to_core, gsum, keep, *sends = call(
+    part = ((size, chans), BF16)
+    to_core, gsum, keep, *sends, first = call(
         functools.partial(slope_body, 256),
         [back.reshape(flat), from_next.reshape(flat), from_prev.reshape(flat), factor, grads, weight, flipped],
-        [(flat, BF16), (flat, F32), ((size, chans), F32)] + [((size, chans), BF16)] * len(others),
+        [(flat, BF16), (flat, F32), ((size, chans), F32)] + [part] * len(others),
         [pltpu.VMEM(flat, BF16), pltpu.VMEM((depth, chans), F32)],
-        flops=4 * rows * depth * chans,
-        nbytes=8 * rows * chans,
+        cost=SLOPE_COST,
+        waits=[prev_low],
+        carried=[first],
     )
     arrived = [to_partner(s, *at) for s, at in zip(sends, others)]
-    high_now, _ = lax.optimization_barrier((high_act, keep))
-    prev_high = shift(high_now, "graph", 1)
+    next_first = shift(first, "graph", -1)
     summed = shift(to_core, "tensor", 1)
-    (grad_edges,) = call(grads_body, [gsum, summed], [(flat, BF16)], nbytes=8 * rows * chans)
-
-    def add_up(scale, parts):
-        return call(functools.partial(total_body, scale), parts, [((size, chans), BF16)])[0]
-
+    grad_edges, token = call(grads_body, [gsum, summed], [(flat, BF16), ((8, 128), F32)], cost=GRADS_COST)
+    acc = triplet((0, nblocks), (prev_low, act.reshape(blocks)), mine.reshape(blocks), F32, TRIPLET_COSTS[0])
     scale = float(1.0 / (ndp * edges_in.shape[0] * nz * rows) ** 0.5)
     stages = bits(nz)
-    total = add_up(1.0 if stages else scale, [keep, *arrived])
-    low_now, _ = lax.optimization_barrier((low_act, total))
-    next_low = shift(low_now, "graph", -1)
-    for i, bit in enumerate(stages):
-        swapped = lax.ppermute(total, "graph", [(z, z ^ bit) for z in range(nz)])
-        total = add_up(scale if i + 1 == len(stages) else 1.0, [total, swapped])
-    high_now, _ = lax.optimization_barrier((high_act, total))
-    next_high = shift(high_now, "graph", -1)
+    total, second = call(
+        functools.partial(total_body, 1.0 if stages else scale),
+        [keep, *arrived],
+        [part],
+        cost=SUM_COST,
+        waits=[acc, tick(TICK_COSTS[0], prev_high)],
+        carried=[second],
+    )
+    next_second = shift(second, "graph", -1)
+    acc = triplet((lead,), (prev_high,), acc, F32, TRIPLET_COSTS[1])
+    waits = [token, acc, tick(TICK_COSTS[1], next_first)]
+    for bit in stages:
+        (total,) = call(
+            functools.partial(total_body, scale if bit == stages[-1] else 1.0),
+            [total, swap(total, bit)],
+            [part],
+            cost=SUM_COST,
+            waits=waits,
+        )
     arrived = [to_partner(total, *at) for at in others]
-    (grad_weight,) = call(gather_body, [total, *arrived], [((depth, chans), F32)])
-
-    acc = triplet((nblocks, 0, half), (act, prev_low, prev_high), mine.reshape(blocks), F32)
-    acc = triplet((2 * nblocks,), (next_low,), acc, F32)
-    edges_out = triplet((2 * nblocks + half,), (next_high,), acc, BF16)
+    acc = triplet((2 * nblocks,), (next_first,), acc, F32, TRIPLET_COSTS[2])
+    (grad_weight,) = call(
+        gather_body,
+        [total, *arrived],
+        [((depth, chans), F32)],
+        cost=GATHER_COST,
+    )
+    edges_out = triplet((2 * nblocks + cuts[1],), (next_second,), acc, BF16, TRIPLET_COSTS[3])
     return edges_out.reshape(1, rows, chans), grad_edges[None], grad_weight
 
 

time: 82.8 us -> 65.2 us (0.79)
  waiting for transfers between devices: 48.7 us -> 25.4 us
  starting transfers between devices: 15.7 us -> 21.8 us
  local copies, waits for them, and re-layouts: 3.68 us -> 1.03 us
  Pallas kernels: 13.1 us -> 15.2 us
    ppermute x6, waiting for transfers between devices: 15.1 us -> 3.62 us  [to_partner(): return lax.ppermute(value, ('graph', 'dp'), pairs)]
    ppermute x8 -> x9, waiting for transfers between devices: 28.5 us -> 21.8 us  [shift(): lax.ppermute(value, axis, [(i, (i + steps) % count) for i in range(count)])]
    ppermute x1, waiting for transfers between devices: 5.07 us -> 0.01 us  [swap(): lax.ppermute(value, 'graph', [(z, z ^ bit) for z in range(lax.axis_size('...]
    unnamed x20 -> x14, local copies, waits for them, and re-layouts: 3.64 us -> 0.04 us
    ppermute x6, starting transfers between devices: 7.1 us -> 10.2 us  [to_partner(): return lax.ppermute(value, ('graph', 'dp'), pairs)]
    ppermute x8 -> x9, starting transfers between devices: 7.95 us -> 10.8 us  [shift(): lax.ppermute(value, axis, [(i, (i + steps) % count) for i in range(count)])]
    pallas_call x11 -> x15, Pallas kernels: 13.1 us -> 15.2 us  [call(): pl.pallas_call(kernel, name=getattr(body, 'func', body).__name__, in_spec...]
    slice x1, local copies, waits for them, and re-layouts: 0.03 us -> 1 us  [shards(): prev_rows = shift(mine[:lead * tile], 'graph', 1)]
  transfers between devices with their start and end apart: 15 -> 16, of which waited for: 12 -> 9; matrix products, arithmetic and copies ran while one was open for 0% -> 0% of each run, Pallas kernels for 14% -> 22%
where the time goes in v4:
time: 65.2 us; the launch traced here: 65 us
  waiting for transfers between devices  25.4 us (39%)
  starting transfers between devices  21.8 us (33%)
  Pallas kernels  15.2 us (23%)
  between operations  1.47 us (2%)
  local copies, waits for them, and re-layouts  1.03 us (2%)
    ppermute x9, waiting for transfers between devices, shift(): lax.ppermute(value, axis, [(i, (i + steps) % count) for i in range(count)])  21.8 us
    pallas_call x15, Pallas kernels, call(): pl.pallas_call(kernel, name=getattr(body, 'func', body).__name__, in_spec...  15.2 us
    ppermute x9, starting transfers between devices, shift(): lax.ppermute(value, axis, [(i, (i + steps) % count) for i in range(count)])  10.8 us
    ppermute x6, starting transfers between devices, to_partner(): return lax.ppermute(value, ('graph', 'dp'), pairs)  10.2 us
    ppermute x6, waiting for transfers between devices, to_partner(): return lax.ppermute(value, ('graph', 'dp'), pairs)  3.62 us
  transfers between devices with their start and end apart: 16, of which 9 were waited for; matrix products, arithmetic and copies ran while one was open for 0% of the time, Pallas kernels for 22%

profile of v4, /device:TPU:0, one launch (start us, length us, event | category | flops | bytes accessed | tf_op | source)
XLA Modules:
  0.0 65.0 jit_solution(9692774915937693426)
XLA Ops:
  0.6 1.0 %slice_bitcast_fusion = bf16[640,256]{1,0:T(8,128)(2,1)S(1)} fusion(bf16[1,1024,256]{2,1,0:T(8,128)(2,1)} %param.7), kind=kLoop, calls=%fused_computation | loop fusion | bytes 655360 | tf_op jit(solution)/shard_map/slice | solution.py:257
  1.6 3.1 %collective-permute-start.3 = (bf16[640,256]{1,0:T(8,128)(2,1)S(1)}, bf16[640,256]{1,0:T(8,128)(2,1)S(1)}, u32[]{:S(2)}, u32[]{:S(2)}) collective-permute-start(bf16[640,256]{1,0:T(8,128)(2,1)S(1)} %slice_bitcast_fusion), channel_id=1, source_target_pairs={{0,4},{4,8},{8,12},{12,0},{1,5},{5,9},{9,13},{13,1},{2,6},{6,10},{... | collective-permute-start | bytes 983048 | tf_op jit(solution)/shard_map/ppermute | solution.py:47
  5.4 2.9 %back_body.2.refs_5_ = bf16[8,128,256]{2,1,0:T(8,128)(2,1)} custom-call(s32[1,1]{1,0:T(1,128)S(6)} %copy.14.refs_0_, s32[1,36]{1,0:T(1,128)} %refs_1_.11, s32[1,36]{1,0:T(1,128)} %refs_2_.15, bf16[36,128,128]{2,1,0:T(8,128)(2,1)} %bitcast.17, bf16[8,128,256]{2,1,0:T(8,128)(2,1)} %bitcast.30), custom_call_target="tpu_custom_call" | custom-call | flops 1150000000 | tf_op jit(solution)/shard_map/back_body/pallas_call | solution.py:31
  8.3 2.4 %collective-permute-start = (bf16[8,128,256]{2,1,0:T(8,128)(2,1)}, bf16[8,128,256]{2,1,0:T(8,128)(2,1)S(1)}, u32[]{:S(2)}, u32[]{:S(2)}) collective-permute-start(bf16[8,128,256]{2,1,0:T(8,128)(2,1)} %back_body.2.refs_5_), channel_id=1, source_target_pairs={{0,12},{4,0},{8,4},{12,8},{1,13},{5,1},{9,5},{13,9},{2,14},{6,2},{... | collective-permute-start | bytes 1572872 | tf_op jit(solution)/shard_map/ppermute | solution.py:47
  10.7 3.6 %back_body.3 = (bf16[8,128,256]{2,1,0:T(8,128)(2,1)}, f32[8,128,256]{2,1,0:T(8,128)}) custom-call(s32[1,1]{1,0:T(1,128)S(6)} %copy.14.refs_0_, s32[1,36]{1,0:T(1,128)} %refs_1_.11, s32[1,36]{1,0:T(1,128)} %refs_2_.15, bf16[36,128,128]{2,1,0:T(8,128)(2,1)} %bitcast.18, bf16[8,128,256]{2,1,0:T(8,128)(2,1)} %bitcast.31, bf16[8,128,256]{2,1,0:T(8,128)(2,1)} %back_body.2.refs_5_), custom_call_target="tpu_custom_call" | custom-call | flops 1150000000 | tf_op jit(solution)/shard_map/back_body/pallas_call | solution.py:31
  14.3 0.8 %collective-permute-start.1 = (bf16[8,128,256]{2,1,0:T(8,128)(2,1)}, bf16[8,128,256]{2,1,0:T(8,128)(2,1)S(1)}, u32[]{:S(2)}, u32[]{:S(2)}) collective-permute-start(bf16[8,128,256]{2,1,0:T(8,128)(2,1)} %get-tuple-element.23), channel_id=1, source_target_pairs={{0,4},{4,8},{8,12},{12,0},{1,5},{5,9},{9,13},{13,1},{2,6},{6,10},{... | collective-permute-start | bytes 1572872 | tf_op jit(solution)/shard_map/ppermute | solution.py:47
  17.2 9.3 %collective-permute-done = bf16[8,128,256]{2,1,0:T(8,128)(2,1)S(1)} collective-permute-done((bf16[8,128,256]{2,1,0:T(8,128)(2,1)}, bf16[8,128,256]{2,1,0:T(8,128)(2,1)S(1)}, u32[]{:S(2)}, u32[]{:S(2)}) %collective-permute-start) | collective-permute-done | bytes 524320 | tf_op jit(solution)/shard_map/ppermute | solution.py:47
  26.4 11.2 %collective-permute-done.1 = bf16[8,128,256]{2,1,0:T(8,128)(2,1)S(1)} collective-permute-done((bf16[8,128,256]{2,1,0:T(8,128)(2,1)}, bf16[8,128,256]{2,1,0:T(8,128)(2,1)S(1)}, u32[]{:S(2)}, u32[]{:S(2)}) %collective-permute-start.1) | collective-permute-done | bytes 524320 | tf_op jit(solution)/shard_map/ppermute | solution.py:47
  37.7 0.9 %slope_body.1 = (bf16[1024,256]{1,0:T(8,128)(2,1)S(1)}, f32[1024,256]{1,0:T(8,128)S(1)}, f32[128,256]{1,0:T(8,128)S(1)}, bf16[128,256]{1,0:T(8,128)(2,1)S(1)}, b...) custom-call(f32[1024,256]{1,0:T(8,128)S(1)} %bitcast.28, ...), custom_call_target="tpu_custom_call", output_to_operand_aliasing={{6}: (8, {})} | custom-call | flops 575000000 | tf_op jit(solution)/shard_map/slope_body/pallas_call | solution.py:31
  38.6 2.4 %collective-permute-start.6 = (bf16[128,256]{1,0:T(8,128)(2,1)S(1)}, bf16[128,256]{1,0:T(8,128)(2,1)S(1)}, u32[]{:S(2)}, u32[]{:S(2)}) collective-permute-start(bf16[128,256]{1,0:T(8,128)(2,1)S(1)} %get-tuple-element.29), channel_id=1, source_target_pairs={{0,6},{2,4},{4,2},{6,0},{8,14},{10,12},{12,10},{14,8},{1,7},{3,5},... | collective-permute-start | bytes 196616 | tf_op jit(solution)/shard_map/ppermute | solution.py:178
  41.0 1.1 %collective-permute-start.7 = (bf16[128,256]{1,0:T(8,128)(2,1)S(1)}, bf16[128,256]{1,0:T(8,128)(2,1)S(1)}, u32[]{:S(2)}, u32[]{:S(2)}) collective-permute-start(bf16[128,256]{1,0:T(8,128)(2,1)S(1)} %get-tuple-element.30), channel_id=1, source_target_pairs={{0,2},{2,0},{4,6},{6,4},{8,10},{10,8},{12,14},{14,12},{1,3},{3,1},... | collective-permute-start | bytes 196616 | tf_op jit(solution)/shard_map/ppermute | solution.py:178
  42.1 1.0 %collective-permute-start.10 = (bf16[4,128,256]{2,1,0:T(8,128)(2,1)S(1)}, bf16[4,128,256]{2,1,0:T(8,128)(2,1)S(1)}, u32[]{:S(2)}, u32[]{:S(2)}) collective-permute-start(bf16[4,128,256]{2,1,0:T(8,128)(2,1)S(1)} %get-tuple-element.35), channel_id=1, source_target_pairs={{0,12},{4,0},{8,4},{12,8},{1,13},{5,1},{9,5},{13,9},{2,14},{6,2},{... | collective-permute-start | bytes 786440 | tf_op jit(solution)/shard_map/ppermute | solution.py:47
  43.1 1.6 %triplet_body.4.refs_4_.refs_5_ = f32[8,128,256]{2,1,0:T(8,128)S(1)} custom-call(s32[1,1]{1,0:T(1,128)S(6)} %copy.14.refs_0_, s32[1,36]{1,0:T(1,128)S(1)} %copy-done.5, s32[1,36]{1,0:T(1,128)S(1)} %copy-done.6, bf16[36,128,128]{2,1,0:T(8,128)(2,1)S(1)} %bitcast.19, bf16[5,128,256]{2,1,0:T(8,128)(2,1)S(1)} %bitcast.27, bf16[8,128,256]{2,1,0:T(8,128)(2,1)S(1)} %bitcast.29, ...), custom_call_target="tpu_custom_call" | custom-call | flops 575000000 | tf_op jit(solution)/shard_map/triplet_body/pallas_call | solution.py:31
  45.8 0.8 %collective-permute-start.12 = (bf16[128,256]{1,0:T(8,128)(2,1)S(1)}, bf16[128,256]{1,0:T(8,128)(2,1)S(1)}, u32[]{:S(2)}, u32[]{:S(2)}) collective-permute-start(bf16[128,256]{1,0:T(8,128)(2,1)S(1)} %get-tuple-element.39.refs_0_), channel_id=1, source_target_pairs={{0,8},{4,12},{8,0},{12,4},{1,9},{5,13},{9,1},{13,5},{2,10},{6,14},... | collective-permute-start | bytes 196616 | tf_op jit(solution)/shard_map/ppermute | solution.py:182
  46.6 2.7 %collective-permute-start.9 = (bf16[4,128,256]{2,1,0:T(8,128)(2,1)S(1)}, bf16[4,128,256]{2,1,0:T(8,128)(2,1)S(1)}, u32[]{:S(2)}, u32[]{:S(2)}) collective-permute-start(bf16[4,128,256]{2,1,0:T(8,128)(2,1)S(1)} %get-tuple-element.34), channel_id=1, source_target_pairs={{0,12},{4,0},{8,4},{12,8},{1,13},{5,1},{9,5},{13,9},{2,14},{6,2},{... | collective-permute-start | bytes 786440 | tf_op jit(solution)/shard_map/ppermute | solution.py:47
  49.3 1.0 %triplet_body.5.refs_5_.refs_3_ = f32[8,128,256]{2,1,0:T(8,128)S(1)} custom-call(s32[1,1]{1,0:T(1,128)S(6)} %copy.14.refs_0_, s32[1,36]{1,0:T(1,128)S(1)} %copy-done.5, s32[1,36]{1,0:T(1,128)S(1)} %copy-done.6, bf16[36,128,128]{2,1,0:T(8,128)(2,1)S(1)} %bitcast.20, bf16[3,128,256]{2,1,0:T(8,128)(2,1)S(1)} %collective-permute-done.8.refs_0_.refs_4_, ...), custom_call_target="tpu_custom_call" | custom-call | flops 345000000 | tf_op jit(solution)/shard_map/triplet_body/pallas_call | solution.py:31
  50.2 1.0 %collective-permute-done.10.refs_4_.refs_0_ = bf16[4,128,256]{2,1,0:T(8,128)(2,1)S(1)} collective-permute-done((bf16[4,128,256]{2,1,0:T(8,128)(2,1)S(1)}, bf16[4,128,256]{2,1,0:T(8,128)(2,1)S(1)}, u32[]{:S(2)}, u32[]{:S(2)}) %collective-permute-start.10) | collective-permute-done | bytes 262176 | tf_op jit(solution)/shard_map/ppermute | solution.py:47
  51.3 1.0 %triplet_body.6.refs_5_ = f32[8,128,256]{2,1,0:T(8,128)S(1)} custom-call(s32[1,1]{1,0:T(1,128)S(6)} %copy.14.refs_0_, s32[1,36]{1,0:T(1,128)S(1)} %copy-done.5, s32[1,36]{1,0:T(1,128)S(1)} %copy-done.6, bf16[36,128,128]{2,1,0:T(8,128)(2,1)S(1)} %bitcast.21, bf16[4,128,256]{2,1,0:T(8,128)(2,1)S(1)} %collective-permute-done.10.refs_4_.refs_0_, ...), custom_call_target="tpu_custom_call" | custom-call | flops 345000000 | tf_op jit(solution)/shard_map/triplet_body/pallas_call | solution.py:31
  52.3 0.9 %grads_body.1 = (bf16[1024,256]{1,0:T(8,128)(2,1)}, f32[8,128]{1,0:T(8,128)S(1)}) custom-call(f32[1024,256]{1,0:T(8,128)S(1)} %get-tuple-element.36.refs_0_, bf16[1024,256]{1,0:T(8,128)(2,1)S(1)} %collective-permute-done.11.refs_1_), custom_call_target="tpu_custom_call" | custom-call | flops 575000000 | tf_op jit(solution)/shard_map/grads_body/pallas_call | solution.py:31
  53.2 1.4 %collective-permute-start.15 = (bf16[128,256]{1,0:T(8,128)(2,1)S(1)}, bf16[128,256]{1,0:T(8,128)(2,1)S(1)}, u32[]{:S(2)}, u32[]{:S(2)}) collective-permute-start(bf16[128,256]{1,0:T(8,128)(2,1)S(1)} %total_body.3.refs_0_), channel_id=1, source_target_pairs={{0,2},{2,0},{4,6},{6,4},{8,10},{10,8},{12,14},{14,12},{1,3},{3,1},... | collective-permute-start | bytes 196616 | tf_op jit(solution)/shard_map/ppermute | solution.py:178
  54.6 5.3 %collective-permute-start.14 = (bf16[128,256]{1,0:T(8,128)(2,1)S(1)}, bf16[128,256]{1,0:T(8,128)(2,1)S(1)}, u32[]{:S(2)}, u32[]{:S(2)}) collective-permute-start(bf16[128,256]{1,0:T(8,128)(2,1)S(1)} %total_body.3.refs_0_), channel_id=1, source_target_pairs={{0,6},{2,4},{4,2},{6,0},{8,14},{10,12},{12,10},{14,8},{1,7},{3,5},... | collective-permute-start | bytes 196616 | tf_op jit(solution)/shard_map/ppermute | solution.py:178
  59.9 1.5 %triplet_body.7 = bf16[8,128,256]{2,1,0:T(8,128)(2,1)} custom-call(s32[1,1]{1,0:T(1,128)S(6)} %copy.14.refs_0_, s32[1,36]{1,0:T(1,128)S(1)} %copy-done.5, s32[1,36]{1,0:T(1,128)S(1)} %copy-done.6, bf16[36,128,128]{2,1,0:T(8,128)(2,1)S(1)} %bitcast.22, bf16[4,128,256]{2,1,0:T(8,128)(2,1)S(1)} %collective-permute-done.9.refs_4_, ...), custom_call_target="tpu_custom_call" | custom-call | flops 6899999744 | tf_op jit(solution)/shard_map/triplet_body/pallas_call | solution.py:31
  62.1 2.0 %collective-permute-done.13.refs_1_ = bf16[128,256]{1,0:T(8,128)(2,1)S(1)} collective-permute-done((bf16[128,256]{1,0:T(8,128)(2,1)S(1)}, bf16[128,256]{1,0:T(8,128)(2,1)S(1)}, u32[]{:S(2)}, u32[]{:S(2)}) %collective-permute-start.13) | collective-permute-done | bytes 65568 | tf_op jit(solution)/shard_map/ppermute | solution.py:178
  64.2 0.8 %gather_body.1 = f32[512,256]{1,0:T(8,128)} custom-call(bf16[128,256]{1,0:T(8,128)(2,1)S(1)} %total_body.3.refs_0_, bf16[128,256]{1,0:T(8,128)(2,1)S(1)} %collective-permute-done.13.refs_1_, bf16[128,256]{1,0:T(8,128)(2,1)S(1)} %collective-permute-done.14.refs_2_, bf16[128,256]{1,0:T(8,128)(2,1)S(1)} %collective-permute-done.15.refs_3_), custom_call_target="tpu_custom_call" | custom-call | flops 3449999872 | tf_op jit(solution)/shard_map/gather_body/pallas_call | solution.py:31
  (38 shorter events, 3.9 us)
Async XLA Ops:
  1.6 13.5 %collective-permute-start.3 = (bf16[640,256]{1,0:T(8,128)(2,1)S(1)}, bf16[640,256]{1,0:T(8,128)(2,1)S(1)}, u32[]{:S(2)}, u32[]{:S(2)}) collective-permute-start(bf16[640,256]{1,0:T(8,128)(2,1)S(1)} %slice_bitcast_fusion), channel_id=1, source_target_pairs={{0,4},{4,8},{8,12},{12,0},{1,5},{5,9},{9,13},{13,1},{2,6},{6,10},{... | collective-permute-start | bytes 983048 | tf_op jit(solution)/shard_map/ppermute | solution.py:47
  4.7 10.5 %collective-permute-start.2 = (bf16[1024,256]{1,0:T(8,128)(2,1)}, bf16[1024,256]{1,0:T(8,128)(2,1)S(1)}, u32[]{:S(2)}, u32[]{:S(2)}) collective-permute-start(bf16[1024,256]{1,0:T(8,128)(2,1)} %bitcast.23), channel_id=1, source_target_pairs={{0,1},{1,0},{2,3},{3,2},{4,5},{5,4},{6,7},{7,6},{8,9},{9,8},{10,11... | collective-permute-start | bytes 1572872 | tf_op jit(solution)/shard_map/ppermute | solution.py:47
  8.2 6.9 %copy-start.1 = (bf16[1,1024,256]{2,1,0:T(8,128)(2,1)S(1)}, bf16[1,1024,256]{2,1,0:T(8,128)(2,1)}, u32[]{:S(2)}) copy-start(bf16[1,1024,256]{2,1,0:T(8,128)(2,1)} %param.7) | copy-start | bytes 1572868
  8.2 6.9 %copy-start.4 = (bf16[512,256]{1,0:T(8,128)(2,1)S(1)}, bf16[512,256]{1,0:T(8,128)(2,1)}, u32[]{:S(2)}) copy-start(bf16[512,256]{1,0:T(8,128)(2,1)} %refs_5_.1) | copy-start | bytes 786436
  8.3 18.1 %collective-permute-start = (bf16[8,128,256]{2,1,0:T(8,128)(2,1)}, bf16[8,128,256]{2,1,0:T(8,128)(2,1)S(1)}, u32[]{:S(2)}, u32[]{:S(2)}) collective-permute-start(bf16[8,128,256]{2,1,0:T(8,128)(2,1)} %back_body.2.refs_5_), channel_id=1, source_target_pairs={{0,12},{4,0},{8,4},{12,8},{1,13},{5,1},{9,5},{13,9},{2,14},{6,2},{... | collective-permute-start | bytes 1572872 | tf_op jit(solution)/shard_map/ppermute | solution.py:47
  14.3 23.4 %collective-permute-start.1 = (bf16[8,128,256]{2,1,0:T(8,128)(2,1)}, bf16[8,128,256]{2,1,0:T(8,128)(2,1)S(1)}, u32[]{:S(2)}, u32[]{:S(2)}) collective-permute-start(bf16[8,128,256]{2,1,0:T(8,128)(2,1)} %get-tuple-element.23), channel_id=1, source_target_pairs={{0,4},{4,8},{8,12},{12,0},{1,5},{5,9},{9,13},{13,1},{2,6},{6,10},{... | collective-permute-start | bytes 1572872 | tf_op jit(solution)/shard_map/ppermute | solution.py:47
  15.2 1.6 %collective-permute-start.4 = (bf16[640,256]{1,0:T(8,128)(2,1)S(1)}, bf16[640,256]{1,0:T(8,128)(2,1)S(1)}, u32[]{:S(2)}, u32[]{:S(2)}) collective-permute-start(bf16[640,256]{1,0:T(8,128)(2,1)S(1)} %collective-permute-done.3.refs_0_), channel_id=1, source_target_pairs={{0,1},{1,0},{2,3},{3,2},{4,5},{5,4},{6,7},{7,6},{8,9},{9,8},{10,11... | collective-permute-start | bytes 983048 | tf_op jit(solution)/shard_map/ppermute | solution.py:47
  15.9 21.7 %copy-start.2 = (f32[8,128,256]{2,1,0:T(8,128)S(1)}, f32[8,128,256]{2,1,0:T(8,128)}, u32[]{:S(2)}) copy-start(f32[8,128,256]{2,1,0:T(8,128)} %get-tuple-element.22) | copy-start | bytes 3145732
  15.9 21.7 %copy-start.3 = (bf16[1,1024,256]{2,1,0:T(8,128)(2,1)S(1)}, bf16[1,1024,256]{2,1,0:T(8,128)(2,1)}, u32[]{:S(2)}) copy-start(bf16[1,1024,256]{2,1,0:T(8,128)(2,1)} %param.13) | copy-start | bytes 1572868
  15.9 28.8 %collective-permute-start.8 = (bf16[3,128,256]{2,1,0:T(8,128)(2,1)S(1)}, bf16[3,128,256]{2,1,0:T(8,128)(2,1)S(1)}, u32[]{:S(2)}, u32[]{:S(2)}) collective-permute-start(bf16[3,128,256]{2,1,0:T(8,128)(2,1)S(1)} %bitcast.37), channel_id=1, source_target_pairs={{0,4},{4,8},{8,12},{12,0},{1,5},{5,9},{9,13},{13,1},{2,6},{6,10},{... | collective-permute-start | bytes 589832 | tf_op jit(solution)/shard_map/ppermute | solution.py:47
  37.6 5.5 %copy-start = (bf16[1,36,128,128]{3,2,1,0:T(8,128)(2,1)S(1)}, bf16[1,36,128,128]{3,2,1,0:T(8,128)(2,1)}, u32[]{:S(2)}) copy-start(bf16[1,36,128,128]{3,2,1,0:T(8,128)(2,1)} %param.9) | copy-start | bytes 3538948
  37.6 5.5 %copy-start.5 = (s32[1,36]{1,0:T(1,128)S(1)}, s32[1,36]{1,0:T(1,128)}, u32[]{:S(2)}) copy-start(s32[1,36]{1,0:T(1,128)} %refs_1_.11) | copy-start | bytes 436
  37.7 5.5 %copy-start.6 = (s32[1,36]{1,0:T(1,128)S(1)}, s32[1,36]{1,0:T(1,128)}, u32[]{:S(2)}) copy-start(s32[1,36]{1,0:T(1,128)} %refs_2_.15) | copy-start | bytes 436
  38.6 6.3 %collective-permute-start.5 = (bf16[128,256]{1,0:T(8,128)(2,1)S(1)}, bf16[128,256]{1,0:T(8,128)(2,1)S(1)}, u32[]{:S(2)}, u32[]{:S(2)}) collective-permute-start(bf16[128,256]{1,0:T(8,128)(2,1)S(1)} %get-tuple-element.28), channel_id=1, source_target_pairs={{0,4},{2,6},{4,0},{6,2},{8,12},{10,14},{12,8},{14,10},{1,5},{3,7},... | collective-permute-start | bytes 196616 | tf_op jit(solution)/shard_map/ppermute | solution.py:178
  38.6 6.8 %collective-permute-start.6 = (bf16[128,256]{1,0:T(8,128)(2,1)S(1)}, bf16[128,256]{1,0:T(8,128)(2,1)S(1)}, u32[]{:S(2)}, u32[]{:S(2)}) collective-permute-start(bf16[128,256]{1,0:T(8,128)(2,1)S(1)} %get-tuple-element.29), channel_id=1, source_target_pairs={{0,6},{2,4},{4,2},{6,0},{8,14},{10,12},{12,10},{14,8},{1,7},{3,5},... | collective-permute-start | bytes 196616 | tf_op jit(solution)/shard_map/ppermute | solution.py:178
  41.0 4.7 %collective-permute-start.7 = (bf16[128,256]{1,0:T(8,128)(2,1)S(1)}, bf16[128,256]{1,0:T(8,128)(2,1)S(1)}, u32[]{:S(2)}, u32[]{:S(2)}) collective-permute-start(bf16[128,256]{1,0:T(8,128)(2,1)S(1)} %get-tuple-element.30), channel_id=1, source_target_pairs={{0,2},{2,0},{4,6},{6,4},{8,10},{10,8},{12,14},{14,12},{1,3},{3,1},... | collective-permute-start | bytes 196616 | tf_op jit(solution)/shard_map/ppermute | solution.py:178
  42.1 9.2 %collective-permute-start.10 = (bf16[4,128,256]{2,1,0:T(8,128)(2,1)S(1)}, bf16[4,128,256]{2,1,0:T(8,128)(2,1)S(1)}, u32[]{:S(2)}, u32[]{:S(2)}) collective-permute-start(bf16[4,128,256]{2,1,0:T(8,128)(2,1)S(1)} %get-tuple-element.35), channel_id=1, source_target_pairs={{0,12},{4,0},{8,4},{12,8},{1,13},{5,1},{9,5},{13,9},{2,14},{6,2},{... | collective-permute-start | bytes 786440 | tf_op jit(solution)/shard_map/ppermute | solution.py:47
  44.7 7.6 %collective-permute-start.11 = (bf16[1024,256]{1,0:T(8,128)(2,1)S(1)}, bf16[1024,256]{1,0:T(8,128)(2,1)S(1)}, u32[]{:S(2)}, u32[]{:S(2)}) collective-permute-start(bf16[1024,256]{1,0:T(8,128)(2,1)S(1)} %get-tuple-element.37), channel_id=1, source_target_pairs={{0,1},{1,0},{2,3},{3,2},{4,5},{5,4},{6,7},{7,6},{8,9},{9,8},{10,11... | collective-permute-start | bytes 1572872 | tf_op jit(solution)/shard_map/ppermute | solution.py:47
  45.8 7.4 %collective-permute-start.12 = (bf16[128,256]{1,0:T(8,128)(2,1)S(1)}, bf16[128,256]{1,0:T(8,128)(2,1)S(1)}, u32[]{:S(2)}, u32[]{:S(2)}) collective-permute-start(bf16[128,256]{1,0:T(8,128)(2,1)S(1)} %get-tuple-element.39.refs_0_), channel_id=1, source_target_pairs={{0,8},{4,12},{8,0},{12,4},{1,9},{5,13},{9,1},{13,5},{2,10},{6,14},... | collective-permute-start | bytes 196616 | tf_op jit(solution)/shard_map/ppermute | solution.py:182
  46.6 13.3 %collective-permute-start.9 = (bf16[4,128,256]{2,1,0:T(8,128)(2,1)S(1)}, bf16[4,128,256]{2,1,0:T(8,128)(2,1)S(1)}, u32[]{:S(2)}, u32[]{:S(2)}) collective-permute-start(bf16[4,128,256]{2,1,0:T(8,128)(2,1)S(1)} %get-tuple-element.34), channel_id=1, source_target_pairs={{0,12},{4,0},{8,4},{12,8},{1,13},{5,1},{9,5},{13,9},{2,14},{6,2},{... | collective-permute-start | bytes 786440 | tf_op jit(solution)/shard_map/ppermute | solution.py:47
  53.2 8.2 %collective-permute-start.15 = (bf16[128,256]{1,0:T(8,128)(2,1)S(1)}, bf16[128,256]{1,0:T(8,128)(2,1)S(1)}, u32[]{:S(2)}, u32[]{:S(2)}) collective-permute-start(bf16[128,256]{1,0:T(8,128)(2,1)S(1)} %total_body.3.refs_0_), channel_id=1, source_target_pairs={{0,2},{2,0},{4,6},{6,4},{8,10},{10,8},{12,14},{14,12},{1,3},{3,1},... | collective-permute-start | bytes 196616 | tf_op jit(solution)/shard_map/ppermute | solution.py:178
  54.6 7.6 %collective-permute-start.14 = (bf16[128,256]{1,0:T(8,128)(2,1)S(1)}, bf16[128,256]{1,0:T(8,128)(2,1)S(1)}, u32[]{:S(2)}, u32[]{:S(2)}) collective-permute-start(bf16[128,256]{1,0:T(8,128)(2,1)S(1)} %total_body.3.refs_0_), channel_id=1, source_target_pairs={{0,6},{2,4},{4,2},{6,0},{8,14},{10,12},{12,10},{14,8},{1,7},{3,5},... | collective-permute-start | bytes 196616 | tf_op jit(solution)/shard_map/ppermute | solution.py:178
  59.9 4.3 %collective-permute-start.13 = (bf16[128,256]{1,0:T(8,128)(2,1)S(1)}, bf16[128,256]{1,0:T(8,128)(2,1)S(1)}, u32[]{:S(2)}, u32[]{:S(2)}) collective-permute-start(bf16[128,256]{1,0:T(8,128)(2,1)S(1)} %total_body.3.refs_0_), channel_id=1, source_target_pairs={{0,4},{2,6},{4,0},{6,2},{8,12},{10,14},{12,8},{14,10},{1,5},{3,7},... | collective-permute-start | bytes 196616 | tf_op jit(solution)/shard_map/ppermute | solution.py:178
